TPU v7x, 32 devices: a whole 2x2x4 slice. The times are simulated.
32 devices in a mesh: groups: 2 (over y), dp: 4 (over z), tensor: 4 (over x, core).
Axes of the slice: x: 2, y: 2, z: 4, core: 2. Of those that a mesh axis runs over, the one named last changes fastest.
Arguments:
- acts: bfloat16 [64, 128, 8192], P(('groups', 'dp'), None, 'tensor'), parts along dimension 0, may hold values from -6 to 6
- grads: bfloat16 [64, 128, 8192], P(('groups', 'dp'), None, 'tensor'), parts along dimension 0, may hold values from -6 to 6
- basis_in: bfloat16 [64, 8192], P(None, 'tensor'), may hold values from -0.0625 to 0.0625
- basis_out: bfloat16 [64, 8192], P(None, 'tensor'), may hold values from -0.0625 to 0.0625
- queries: bfloat16 [512, 4096], P(('groups', 'dp')), parts along dimension 0, may hold values from -6 to 6
Outputs:
- scores: float32 [64, 256], P(('groups', 'dp', 'tensor')), parts along dimension 0
There are 2 independent parts, one for each index of `groups`. A program takes and returns all parts, laid end to end along the dimension named above; an argument that names none is the same for every part. Nothing has to cross between parts.
All inputs are finite; a program needn't handle non-finite values.
Results may differ from a plain program's by a relative error of at most 0.003.
Values may be sent and summed in bfloat16 or wider, within the bound.
No kernel may reach another device: no remote copies, remote signals or barrier semaphores. Data moves between devices by JAX's collectives and lax.ppermute only.
A program may use at most 64 MiB of HBM per device.

v0:
```python
import jax
import jax.numpy as jnp
from jax import lax
from jax.sharding import PartitionSpec as P


def local(acts, grads, basis_in, basis_out, queries):
    rank = basis_in.shape[0]
    length = acts.shape[1]
    left = jnp.einsum("slh,rh->slr", acts, basis_in, preferred_element_type=jnp.float32)
    right = jnp.einsum("slh,rh->slr", grads, basis_out, preferred_element_type=jnp.float32)
    joined = jnp.concatenate([left, right], axis=2)
    owned = acts.shape[0] // lax.axis_size("tensor")
    summed = lax.psum_scatter(joined, "tensor", scatter_dimension=0, tiled=True)
    outer = (
        jnp.einsum(
            "slr,slq->srq",
            summed[:, :, :rank],
            summed[:, :, rank:],
            precision=lax.Precision.HIGHEST,
        )
        / length
    )
    sketch = outer.reshape(owned, rank * rank).astype(jnp.bfloat16)
    return (
        lax.dot_general(
            sketch,
            lax.all_gather(queries, "dp", axis=0, tiled=True),
            (((1,), (1,)), ((), ())),
            preferred_element_type=jnp.float32,
        )
        / rank
    )


def solution(mesh):
    in_specs = (
        P(("groups", "dp"), None, "tensor"),
        P(("groups", "dp"), None, "tensor"),
        P(None, "tensor"),
        P(None, "tensor"),
        P(("groups", "dp"), None),
    )
    out_specs = P(("groups", "dp", "tensor"), None)
    return jax.shard_map(local, mesh=mesh, in_specs=in_specs, out_specs=out_specs, check_vma=False)
```

profile of v0, /device:TPU:0, one launch (start us, length us, event | category | flops | bytes accessed | tf_op | source)
XLA Modules:
  0.0 75.0 jit_solution(11406747308760830555)
XLA Ops:
  7.4 0.0 copy-start
  7.4 0.0 copy-start.2
  7.4 0.0 reduce-scatter.2.cloned.1.call-start
  7.4 0.9 %copy-done = bf16[64,2048]{1,0:T(8,128)(2,1)S(1)} copy-done((bf16[64,2048]{1,0:T(8,128)(2,1)S(1)}, bf16[64,2048]{1,0:T(8,128)(2,1)}, u32[]{:S(2)}) %copy-start) | copy-done | bytes 262168
  8.3 0.0 copy-start.1
  8.3 3.7 %fusion.1 = f32[8,128,64]{1,2,0:T(8,128)S(1)} fusion(bf16[8,128,2048]{2,1,0:T(8,128)(2,1)} %param.6, bf16[64,2048]{1,0:T(8,128)(2,1)S(1)} %copy-done), kind=kOutput, calls=%fused_computation.4 | convolution fusion | flops 268435456 | bytes 4718592 | tf_op jit(solution)/shard_map/slh,rh->slr/dot_general | solution.py:11
  12.0 0.0 copy-done.2
  12.1 0.0 copy-done.1
  12.1 1.4 %fusion.3 = f32[8,128,64]{1,2,0:T(8,128)S(1)} fusion(bf16[8,128,2048]{2,1,0:T(8,128)(2,1)S(1)} %copy-done.1, bf16[64,2048]{1,0:T(8,128)(2,1)S(1)} %copy-done.2), kind=kOutput, calls=%fused_computation.6 | convolution fusion | flops 268435456 | bytes 4718592 | tf_op jit(solution)/shard_map/slh,rh->slr/dot_general | solution.py:10
  13.5 0.8 %pad_maximum_fusion = f32[8,128,128]{1,2,0:T(8,128)} fusion(f32[8,128,64]{1,2,0:T(8,128)S(1)} %fusion.1, f32[8,128,64]{1,2,0:T(8,128)S(1)} %fusion.3), kind=kLoop, calls=%fused_computation.3 | loop fusion | flops 131072 | bytes 1048576 | tf_op jit(solution)/shard_map/concatenate | solution.py:12
  14.3 0.0 reduce-scatter.2.cloned.1.call-update
  14.3 0.0 all-gather.2.cloned.1.call-start
  14.4 0.5 all-gather.2.cloned.1.call-update
  14.9 24.0 %reduce-scatter.2.cloned.1.call-done = f32[2,128,128]{1,2,0:T(8,128)} async-done(((f32[8,128,128]{1,2,0:T(8,128)}), f32[2,128,128]{1,2,0:T(8,128)}) %reduce-scatter.2.cloned.1.call-update) | async-done | bytes 131088 | tf_op jit(solution)/shard_map/reduce_scatter | solution.py:14
  38.9 1.1 %fusion = bf16[2,64,64]{2,1,0:T(8,128)(2,1)S(1)} fusion(f32[2,128,128]{1,2,0:T(8,128)} %reduce-scatter.2.cloned.1.call-done), kind=kOutput, calls=%fused_computation.1 | convolution fusion | flops 12599296 | bytes 147456 | tf_op jit(solution)/shard_map/slr,slq->srq/dot_general | solution.py:16
  40.0 0.1 convert_element_type.7
  40.1 24.7 %all-gather.2.cloned.1.call-done = bf16[256,4096]{1,0:T(8,128)(2,1)} async-done(((bf16[64,4096]{1,0:T(8,128)(2,1)}), bf16[256,4096]{1,0:T(8,128)(2,1)}) %all-gather.2.cloned.1.call-update) | async-done | bytes 2097168 | tf_op jit(solution)/shard_map/all_gather | solution.py:28
  64.7 2.8 %convolution_multiply_fusion.1 = f32[2,256]{1,0:T(2,128)} fusion(bf16[2,4096]{1,0:T(2,128)(2,1)S(1)} %convert_element_type.7, bf16[256,4096]{1,0:T(8,128)(2,1)} %all-gather.2.cloned.1.call-done), kind=kOutput, calls=%fused_computation.2 | convolution fusion | flops 4194816 | bytes 2115584 | tf_op jit(solution)/shard_map/dot_general | solution.py:26
Async XLA Ops:
  7.4 1.0 %copy-start = (bf16[64,2048]{1,0:T(8,128)(2,1)S(1)}, bf16[64,2048]{1,0:T(8,128)(2,1)}, u32[]{:S(2)}) copy-start(bf16[64,2048]{1,0:T(8,128)(2,1)} %param.8) | copy-start | bytes 786436
  7.4 4.7 %copy-start.2 = (bf16[64,2048]{1,0:T(8,128)(2,1)S(1)}, bf16[64,2048]{1,0:T(8,128)(2,1)}, u32[]{:S(2)}) copy-start(bf16[64,2048]{1,0:T(8,128)(2,1)} %param.7) | copy-start | bytes 786436
  7.4 31.5 %reduce-scatter.2.cloned.1.call-start = ((), (), s32[]{:S(2)}) async-start(), calls=%async_computation.1 | async-start | bytes 655360 | tf_op jit(solution)/shard_map/reduce_scatter | solution.py:14
  8.3 3.7 %copy-start.1 = (bf16[8,128,2048]{2,1,0:T(8,128)(2,1)S(1)}, bf16[8,128,2048]{2,1,0:T(8,128)(2,1)}, u32[]{:S(2)}) copy-start(bf16[8,128,2048]{2,1,0:T(8,128)(2,1)} %param.5) | copy-start | bytes 12582916
  14.3 50.4 %all-gather.2.cloned.1.call-start = ((), (), s32[]{:S(2)}) async-start(), calls=%async_computation.2 | async-start | bytes 2621440 | tf_op jit(solution)/shard_map/all_gather | solution.py:28
Sparse Core Ops, SparseCore 0:
  14.4 24.3 reduce-scatter.1
Sparse Core Ops, SparseCore 1:
  16.4 48.2 all-gather.1
where the time goes:
time: 75.2 us; the launch traced here: 75 us
  waiting for transfers between devices  49.2 us (65%)
  between operations  14.9 us (20%)
  matrix products  9.05 us (12%)
  local copies, waits for them, and re-layouts  1.05 us (1%)
  other arithmetic  0.85 us (1%)
    all_gather x1, waiting for transfers between devices, local(): lax.all_gather(queries, 'dp', axis=0, tiled=True)  24.7 us
    reduce_scatter x1, waiting for transfers between devices, local(): summed = lax.psum_scatter(joined, 'tensor', scatter_dimension=0, tiled=True)  24 us
    dot_general x1, matrix products, local(): jnp.einsum('slh,rh->slr', grads, basis_out, preferred_element_type=jnp.fl...  3.73 us
    dot_general x1, matrix products, local(): lax.dot_general(sketch, lax.all_gather(queries, 'dp', axis=0, tiled=True)...  2.82 us
  transfers between devices with their start and end apart: 2, of which 2 were waited for; matrix products, arithmetic and copies ran while one was open for 2% of the time, Pallas kernels for 0%

commit v1 on v0

v1 whole, which is shorter than its diff:
```python
import jax
import jax.numpy as jnp
from jax import lax
from jax.sharding import PartitionSpec as P

BF, F32 = jnp.bfloat16, jnp.float32


def local(acts, grads, basis_in, basis_out, queries):
    rank = basis_in.shape[0]
    length = acts.shape[1]
    nt, nd = lax.axis_size("tensor"), lax.axis_size("dp")
    nx, no = nt // 2, nd // 2
    t, d = lax.axis_index("tensor"), lax.axis_index("dp")
    x, c = t // 2, t % 2
    o, i = d // 2, d % 2
    own = acts.shape[0] // nt
    nq = queries.shape[0]
    core = [(k, k ^ 1) for k in range(nt)]

    def xshift(k):
        return [(a * 2 + b, ((a + k) % nx) * 2 + b) for a in range(nx) for b in range(2)]

    def oshift(k):
        return [(a * 2 + b, ((a + k) % no) * 2 + b) for a in range(no) for b in range(2)]

    near = [(k, k ^ 1) for k in range(nd)]

    half = nq // 2
    part = lax.dynamic_slice_in_dim(queries, c * half, half, 0)
    far_mine = lax.ppermute(part, "dp", near)
    far_other = lax.ppermute(far_mine, "tensor", core)

    left = jnp.einsum("slh,rh->slr", acts, basis_in, preferred_element_type=F32)
    right = jnp.einsum("slh,rh->slr", grads, basis_out, preferred_element_type=F32)
    joined = jnp.concatenate([left, right], axis=2).reshape(nx, 2, own, length, 2 * rank)
    give = lax.dynamic_index_in_dim(joined, 1 - c, 1, False)
    keep = lax.dynamic_index_in_dim(joined, c, 1, False)
    keep = keep + lax.ppermute(give, "tensor", core)
    mine = lax.dynamic_index_in_dim(keep, x, 0, False)
    for k in range(1, nx):
        give = lax.dynamic_index_in_dim(keep, (x + k) % nx, 0, False).astype(BF)
        mine = mine + lax.ppermute(give, "tensor", xshift(k)).astype(F32)
    outer = jnp.einsum("slr,slq->srq", mine[:, :, :rank], mine[:, :, rank:], precision=lax.Precision.HIGHEST)
    sketch = outer.reshape(own, rank * rank) / (length * rank)

    hi = sketch.astype(BF)
    lo = (sketch - hi.astype(F32)).astype(BF)
    rows = jnp.concatenate([hi, lo], 0)
    all_rows = [rows] + [lax.ppermute(rows, "dp", oshift(k)) for k in range(1, no)]
    stacked = jnp.concatenate(all_rows, 0)

    def score(q):
        s = lax.dot_general(stacked, q, (((1,), (1,)), ((), ())), preferred_element_type=F32)
        s = s.reshape(no, 2, own, -1)
        return s[:, 0] + s[:, 1]

    near_s = score(queries)
    fm, fo = score(far_mine), score(far_other)
    lohalf, hihalf = jnp.where(c == 0, fm, fo), jnp.where(c == 0, fo, fm)
    far_s = jnp.concatenate([lohalf, hihalf], 2)
    first = jnp.where(i == 0, near_s, far_s)
    second = jnp.where(i == 0, far_s, near_s)
    both = jnp.concatenate([first, second], 2)
    blocks = [both[0]] + [lax.ppermute(both[k], "dp", oshift(no - k)) for k in range(1, no)]
    allb = jnp.stack(blocks, 0)
    allb = jnp.roll(allb, o, axis=0) if no > 2 else jnp.where(o == 0, allb, allb[::-1])
    return jnp.swapaxes(allb, 0, 1).reshape(own, nd * nq)


def solution(mesh):
    in_specs = (
        P(("groups", "dp"), None, "tensor"),
        P(("groups", "dp"), None, "tensor"),
        P(None, "tensor"),
        P(None, "tensor"),
        P(("groups", "dp"), None),
    )
    out_specs = P(("groups", "dp", "tensor"), None)
    return jax.shard_map(local, mesh=mesh, in_specs=in_specs, out_specs=out_specs, check_vma=False)
```

time: 75.2 us -> 25.9 us (0.34)
  waiting for transfers between devices: 49.2 us -> 8.22 us
  between operations: 14.9 us -> 0.09 us
  starting transfers between devices: 0.05 us -> 10.4 us
  matrix products: 9.05 us -> 5.98 us
  local copies, waits for them, and re-layouts: 1.05 us -> 0.17 us
    all_gather x1 -> x0, waiting for transfers between devices: 24.7 us -> none  [local(): lax.all_gather(queries, 'dp', axis=0, tiled=True)]
    reduce_scatter x1 -> x0, waiting for transfers between devices: 24 us -> none  [local(): summed = lax.psum_scatter(joined, 'tensor', scatter_dimension=0, tiled=True)]
    ppermute x0 -> x6, starting transfers between devices: none -> 10.4 us  [the longest x1 3.04 us: local(): lax.ppermute(rows, 'dp', oshift(k))]
    ppermute x0 -> x6, waiting for transfers between devices: none -> 8.22 us  [the longest x1 3 us: local(): far_mine = lax.ppermute(part, 'dp', near)]
    dot_general x4 -> x6, matrix products: 9.05 us -> 5.98 us  [the longest x1 3.75 us: local(): jnp.einsum('slh,rh->slr', grads, basis_out, preferred_element_type=F32)]
    unnamed x6, local copies, waits for them, and re-layouts: 0.95 us -> 0.01 us
  transfers between devices with their start and end apart: 2 -> 6, of which waited for: 2 -> 5; matrix products, arithmetic and copies ran while one was open for 2% -> 3% of each run, Pallas kernels for 0% -> 0%
where the time goes in v1:
time: 25.9 us; the launch traced here: 25.7 us
  starting transfers between devices  10.4 us (40%)
  waiting for transfers between devices  8.22 us (32%)
  matrix products  5.98 us (23%)
  other arithmetic  0.89 us (3%)
    dot_general x1, matrix products, local(): jnp.einsum('slh,rh->slr', grads, basis_out, preferred_element_type=F32)  3.75 us
    ppermute x1, starting transfers between devices, local(): lax.ppermute(rows, 'dp', oshift(k))  3.04 us
    ppermute x1, waiting for transfers between devices, local(): far_mine = lax.ppermute(part, 'dp', near)  3 us
    ppermute x1, starting transfers between devices, local(): mine = mine + lax.ppermute(give, 'tensor', xshift(k)).astype(F32)  2.93 us
    ppermute x1, starting transfers between devices, local(): lax.ppermute(both[k], 'dp', oshift(no - k))  2.25 us
    ppermute x1, waiting for transfers between devices, local(): lax.ppermute(both[k], 'dp', oshift(no - k))  2.23 us
    ppermute x1, starting transfers between devices, local(): far_mine = lax.ppermute(part, 'dp', near)  1.64 us
    dot_general x1, matrix products, local(): left = jnp.einsum('slh,rh->slr', acts, basis_in, preferred_element_type=F32)  1.39 us
  transfers between devices with their start and end apart: 6, of which 5 were waited for; matrix products, arithmetic and copies ran while one was open for 3% of the time, Pallas kernels for 0%

profile of v1, /device:TPU:0, one launch (start us, length us, event | category | flops | bytes accessed | tf_op | source)
XLA Modules:
  0.0 25.7 jit_solution(2587278664677883141)
XLA Ops:
  0.0 0.0 copy-start
  0.0 0.0 copy-start.2
  0.0 0.0 copy-start.1
  0.0 3.8 %fusion = f32[8,128,64]{1,2,0:T(8,128)S(1)} fusion(bf16[8,128,2048]{2,1,0:T(8,128)(2,1)} %param.6, bf16[64,2048]{1,0:T(8,128)(2,1)} %param.8), kind=kOutput, calls=%fused_computation.3 | convolution fusion | flops 268435456 | bytes 4718592 | tf_op jit(solution)/shard_map/slh,rh->slr/dot_general | solution.py:35
  3.8 0.0 copy-done.2
  3.8 0.0 copy-done.1
  3.8 1.4 %fusion.2 = f32[8,128,64]{1,2,0:T(8,128)S(1)} fusion(bf16[8,128,2048]{2,1,0:T(8,128)(2,1)S(1)} %copy-done.1, bf16[64,2048]{1,0:T(8,128)(2,1)S(1)} %copy-done.2), kind=kOutput, calls=%fused_computation.5 | convolution fusion | flops 268435456 | bytes 4718592 | tf_op jit(solution)/shard_map/slh,rh->slr/dot_general | solution.py:34
  5.2 0.5 %collective-permute-start = (f32[2,2,128,128]{2,3,1,0:T(8,128)S(1)}, f32[2,2,128,128]{2,3,1,0:T(8,128)S(1)}, u32[]{:S(2)}, u32[]{:S(2)}) collective-permute-start(f32[2,2,128,128]{2,3,1,0:T(8,128)S(1)} %dynamic-slice_bitcast_fusion), channel_id=1, source_target_pairs={{0,1},{1,0},{2,3},{3,2},{4,5},{5,4},{6,7},{7,6},{8,9},{9,8},{10,11... | collective-permute-start | bytes 786440 | tf_op jit(solution)/shard_map/ppermute | solution.py:39
  5.8 1.2 %collective-permute-done = f32[2,2,128,128]{2,3,1,0:T(8,128)S(1)} collective-permute-done((f32[2,2,128,128]{2,3,1,0:T(8,128)S(1)}, f32[2,2,128,128]{2,3,1,0:T(8,128)S(1)}, u32[]{:S(2)}, u32[]{:S(2)}) %collective-permute-start) | collective-permute-done | bytes 262176 | tf_op jit(solution)/shard_map/ppermute | solution.py:39
  7.0 2.9 %collective-permute-start.1 = (bf16[2,128,128]{1,2,0:T(8,128)(2,1)S(1)}, bf16[2,128,128]{1,2,0:T(8,128)(2,1)S(1)}, u32[]{:S(2)}, u32[]{:S(2)}) collective-permute-start(bf16[2,128,128]{1,2,0:T(8,128)(2,1)S(1)} %fusion.4), channel_id=1, source_target_pairs={{0,2},{1,3},{2,0},{3,1},{4,6},{5,7},{6,4},{7,5},{8,10},{9,11},{10,... | collective-permute-start | bytes 196616 | tf_op jit(solution)/shard_map/ppermute | solution.py:43
  9.9 0.0 copy-done
  9.9 1.6 %collective-permute-start.3 = (bf16[32,4096]{1,0:T(8,128)(2,1)S(1)}, bf16[32,4096]{1,0:T(8,128)(2,1)S(1)}, u32[]{:S(2)}, u32[]{:S(2)}) collective-permute-start(bf16[32,4096]{1,0:T(8,128)(2,1)S(1)} %constant_dynamic-slice_fusion), channel_id=1, source_target_pairs={{0,4},{4,0},{8,12},{12,8},{1,5},{5,1},{9,13},{13,9},{2,6},{6,2},{1... | collective-permute-start | bytes 786440 | tf_op jit(solution)/shard_map/ppermute | solution.py:31
  11.6 0.7 %collective-permute-done.1 = bf16[2,128,128]{1,2,0:T(8,128)(2,1)S(1)} collective-permute-done((bf16[2,128,128]{1,2,0:T(8,128)(2,1)S(1)}, bf16[2,128,128]{1,2,0:T(8,128)(2,1)S(1)}, u32[]{:S(2)}, u32[]{:S(2)}) %collective-permute-start.1) | collective-permute-done | bytes 65568 | tf_op jit(solution)/shard_map/ppermute | solution.py:43
  12.3 0.2 convolution_multiply_fusion
  12.6 0.1 div.31
  12.7 3.0 %collective-permute-start.2 = (bf16[4,4096]{1,0:T(4,128)(2,1)S(1)}, bf16[4,4096]{1,0:T(4,128)(2,1)S(1)}, u32[]{:S(2)}, u32[]{:S(2)}) collective-permute-start(bf16[4,4096]{1,0:T(4,128)(2,1)S(1)} %pad_maximum_fusion.2), channel_id=1, source_target_pairs={{0,8},{4,12},{8,0},{12,4},{1,9},{5,13},{9,1},{13,5},{2,10},{6,14},... | collective-permute-start | bytes 98312 | tf_op jit(solution)/shard_map/ppermute | solution.py:50
  15.8 3.0 %collective-permute-done.3 = bf16[32,4096]{1,0:T(8,128)(2,1)S(1)} collective-permute-done((bf16[32,4096]{1,0:T(8,128)(2,1)S(1)}, bf16[32,4096]{1,0:T(8,128)(2,1)S(1)}, u32[]{:S(2)}, u32[]{:S(2)}) %collective-permute-start.3) | collective-permute-done | bytes 262176 | tf_op jit(solution)/shard_map/ppermute | solution.py:31
  18.8 0.0 collective-permute-start.4
  18.8 0.0 collective-permute-done.2
  18.8 0.2 fusion.15
  19.0 0.2 fusion.16
  19.2 1.1 %collective-permute-done.4 = bf16[32,4096]{1,0:T(8,128)(2,1)S(1)} collective-permute-done((bf16[32,4096]{1,0:T(8,128)(2,1)S(1)}, bf16[32,4096]{1,0:T(8,128)(2,1)S(1)}, u32[]{:S(2)}, u32[]{:S(2)}) %collective-permute-start.4) | collective-permute-done | bytes 262176 | tf_op jit(solution)/shard_map/ppermute | solution.py:32
  20.3 0.2 fusion.14
  20.5 0.1 broadcast_select_fusion.1
  20.6 0.1 fusion.12
  20.7 2.2 %collective-permute-start.5 = (f32[2,128]{1,0:T(2,128)S(1)}, f32[2,128]{1,0:T(2,128)S(1)}, u32[]{:S(2)}, u32[]{:S(2)}) collective-permute-start(f32[2,128]{1,0:T(2,128)S(1)} %get-tuple-element.12), channel_id=1, source_target_pairs={{0,8},{4,12},{8,0},{12,4},{1,9},{5,13},{9,1},{13,5},{2,10},{6,14},... | collective-permute-start | bytes 3080 | tf_op jit(solution)/shard_map/ppermute | solution.py:65
  22.9 2.2 %collective-permute-done.5 = f32[2,128]{1,0:T(2,128)S(1)} collective-permute-done((f32[2,128]{1,0:T(2,128)S(1)}, f32[2,128]{1,0:T(2,128)S(1)}, u32[]{:S(2)}, u32[]{:S(2)}) %collective-permute-start.5) | collective-permute-done | bytes 1056 | tf_op jit(solution)/shard_map/ppermute | solution.py:65
  25.1 0.6 %fusion.7 = f32[2,256]{1,0:T(2,128)} fusion(f32[2,2,128]{2,1,0:T(2,128)S(1)} %pad_maximum_fusion.4, pred[]{:T(512)S(6)} %eq.15), kind=kLoop, calls=%fused_computation.17 | loop fusion | flops 512 | bytes 4097 | tf_op jit(solution)/shard_map/reshape | solution.py:68
  (10 shorter events, 0.2 us)
Async XLA Ops:
  0.0 9.9 %copy-start = (bf16[64,4096]{1,0:T(8,128)(2,1)S(1)}, bf16[64,4096]{1,0:T(8,128)(2,1)}, u32[]{:S(2)}) copy-start(bf16[64,4096]{1,0:T(8,128)(2,1)} %param.9) | copy-start | bytes 1572868
  0.0 3.8 %copy-start.2 = (bf16[64,2048]{1,0:T(8,128)(2,1)S(1)}, bf16[64,2048]{1,0:T(8,128)(2,1)}, u32[]{:S(2)}) copy-start(bf16[64,2048]{1,0:T(8,128)(2,1)} %param.7) | copy-start | bytes 786436
  0.0 3.8 %copy-start.1 = (bf16[8,128,2048]{2,1,0:T(8,128)(2,1)S(1)}, bf16[8,128,2048]{2,1,0:T(8,128)(2,1)}, u32[]{:S(2)}) copy-start(bf16[8,128,2048]{2,1,0:T(8,128)(2,1)} %param.5) | copy-start | bytes 12582916
  5.2 1.7 %collective-permute-start = (f32[2,2,128,128]{2,3,1,0:T(8,128)S(1)}, f32[2,2,128,128]{2,3,1,0:T(8,128)S(1)}, u32[]{:S(2)}, u32[]{:S(2)}) collective-permute-start(f32[2,2,128,128]{2,3,1,0:T(8,128)S(1)} %dynamic-slice_bitcast_fusion), channel_id=1, source_target_pairs={{0,1},{1,0},{2,3},{3,2},{4,5},{5,4},{6,7},{7,6},{8,9},{9,8},{10,11... | collective-permute-start | bytes 786440 | tf_op jit(solution)/shard_map/ppermute | solution.py:39
  7.0 5.3 %collective-permute-start.1 = (bf16[2,128,128]{1,2,0:T(8,128)(2,1)S(1)}, bf16[2,128,128]{1,2,0:T(8,128)(2,1)S(1)}, u32[]{:S(2)}, u32[]{:S(2)}) collective-permute-start(bf16[2,128,128]{1,2,0:T(8,128)(2,1)S(1)} %fusion.4), channel_id=1, source_target_pairs={{0,2},{1,3},{2,0},{3,1},{4,6},{5,7},{6,4},{7,5},{8,10},{9,11},{10,... | collective-permute-start | bytes 196616 | tf_op jit(solution)/shard_map/ppermute | solution.py:43
  9.9 8.8 %collective-permute-start.3 = (bf16[32,4096]{1,0:T(8,128)(2,1)S(1)}, bf16[32,4096]{1,0:T(8,128)(2,1)S(1)}, u32[]{:S(2)}, u32[]{:S(2)}) collective-permute-start(bf16[32,4096]{1,0:T(8,128)(2,1)S(1)} %constant_dynamic-slice_fusion), channel_id=1, source_target_pairs={{0,4},{4,0},{8,12},{12,8},{1,5},{5,1},{9,13},{13,9},{2,6},{6,2},{1... | collective-permute-start | bytes 786440 | tf_op jit(solution)/shard_map/ppermute | solution.py:31
  12.7 6.0 %collective-permute-start.2 = (bf16[4,4096]{1,0:T(4,128)(2,1)S(1)}, bf16[4,4096]{1,0:T(4,128)(2,1)S(1)}, u32[]{:S(2)}, u32[]{:S(2)}) collective-permute-start(bf16[4,4096]{1,0:T(4,128)(2,1)S(1)} %pad_maximum_fusion.2), channel_id=1, source_target_pairs={{0,8},{4,12},{8,0},{12,4},{1,9},{5,13},{9,1},{13,5},{2,10},{6,14},... | collective-permute-start | bytes 98312 | tf_op jit(solution)/shard_map/ppermute | solution.py:50
  18.8 1.5 %collective-permute-start.4 = (bf16[32,4096]{1,0:T(8,128)(2,1)S(1)}, bf16[32,4096]{1,0:T(8,128)(2,1)S(1)}, u32[]{:S(2)}, u32[]{:S(2)}) collective-permute-start(bf16[32,4096]{1,0:T(8,128)(2,1)S(1)} %collective-permute-done.3), channel_id=1, source_target_pairs={{0,1},{1,0},{2,3},{3,2},{4,5},{5,4},{6,7},{7,6},{8,9},{9,8},{10,11... | collective-permute-start | bytes 786440 | tf_op jit(solution)/shard_map/ppermute | solution.py:32
  20.7 4.5 %collective-permute-start.5 = (f32[2,128]{1,0:T(2,128)S(1)}, f32[2,128]{1,0:T(2,128)S(1)}, u32[]{:S(2)}, u32[]{:S(2)}) collective-permute-start(f32[2,128]{1,0:T(2,128)S(1)} %get-tuple-element.12), channel_id=1, source_target_pairs={{0,8},{4,12},{8,0},{12,4},{1,9},{5,13},{9,1},{13,5},{2,10},{6,14},... | collective-permute-start | bytes 3080 | tf_op jit(solution)/shard_map/ppermute | solution.py:65

commit v2 on v1

v2 whole, which is shorter than its diff:
```python
import functools

import jax
import jax.numpy as jnp
from jax import lax
from jax.experimental import pallas as pl
from jax.experimental.pallas import tpu as pltpu
from jax.sharding import PartitionSpec as P

BF, F32 = jnp.bfloat16, jnp.float32


def settle_kernel(arrived, held):
    held[...] = arrived[...]


def settle(arrived):
    return pl.pallas_call(
        settle_kernel,
        out_shape=jax.ShapeDtypeStruct(arrived.shape, arrived.dtype),
        in_specs=[pl.BlockSpec(memory_space=pltpu.VMEM)],
        out_specs=pl.BlockSpec(memory_space=pltpu.VMEM),
        compiler_params=pltpu.CompilerParams(vmem_limit_bytes=16 * 2**20),
        cost_estimate=pl.CostEstimate(flops=10000000000, bytes_accessed=0, transcendentals=0),
    )(arrived)


def project_kernel(nx, nt, values, basis, give, keep):
    rows = give.shape[2]
    t = lax.axis_index("tensor")
    x, c = t // 2, t % 2
    for j in range(nt):
        k, other = j % nx, j < nx
        place = lax.rem(x + k, nx) * 2 + ((1 - c) if other else c)
        source = pl.ds(pl.multiple_of(place * rows, rows), rows)
        to = give if other else keep
        to[k] = lax.dot_general(basis[...], values[source], (((1,), (1,)), ((), ())), preferred_element_type=F32)


def project(values, basis, nt):
    rank, hidden = basis.shape
    rows = values.shape[0] // nt
    nx = nt // 2
    shape = jax.ShapeDtypeStruct((nx, rank, rows), F32)
    return pl.pallas_call(
        functools.partial(project_kernel, nx, nt),
        out_shape=[shape, shape],
        in_specs=[pl.BlockSpec(memory_space=pltpu.VMEM)] * 2,
        out_specs=[pl.BlockSpec(memory_space=pltpu.VMEM)] * 2,
        compiler_params=pltpu.CompilerParams(vmem_limit_bytes=16 * 2**20),
        cost_estimate=pl.CostEstimate(flops=2 * nt * rows * hidden * rank, bytes_accessed=2 * nt * rows * hidden, transcendentals=0),
    )(values, basis)


def local(acts, grads, basis_in, basis_out, queries):
    rank = basis_in.shape[0]
    length, hidden = acts.shape[1:]
    nt, nd = lax.axis_size("tensor"), lax.axis_size("dp")
    nx, no = nt // 2, nd // 2
    t, d = lax.axis_index("tensor"), lax.axis_index("dp")
    c = t % 2
    o, i = d // 2, d % 2

    def at(a, b):
        return a * 2 + b

    own = acts.shape[0] // nt
    nq = queries.shape[0]
    core = [(k, k ^ 1) for k in range(nt)]

    def xshift(k):
        return [(a * 2 + b, ((a + k) % nx) * 2 + b) for a in range(nx) for b in range(2)]

    def oshift(k):
        return [(at(a, b), at((a + k) % no, b)) for a in range(no) for b in range(2)]

    near = [(at(a, b), at(a, 1 - b)) for a in range(no) for b in range(2)]

    half, depth = nq // 2, queries.shape[1]
    part = settle(lax.dynamic_slice_in_dim(queries, c * half, half, 0))
    far_mine = lax.ppermute(part, "dp", near)
    acts, grads, part = lax.optimization_barrier((acts, grads, part))

    give_r, keep_r = project(grads.reshape(-1, hidden), basis_out, nt)
    give_l, keep_l = project(acts.reshape(-1, hidden), basis_in, nt)
    got = lax.ppermute(jnp.concatenate([give_l, give_r], 1), "tensor", core)
    keep = jnp.concatenate([keep_l, keep_r], 1) + got
    mine = keep[0]
    groups = [[a * 2 + b for a in range(nx)] for b in range(2)]
    sent = jnp.stack([keep[k] for k in range(1, nx)], 0).astype(BF)
    everyone = lax.all_gather(sent, "tensor", axis=0, axis_index_groups=groups)
    x = t // 2
    for k in range(1, nx):
        mine = mine + lax.dynamic_index_in_dim(everyone, (x - k) % nx, 0, False)[k - 1].astype(F32)
    mine = mine.reshape(2, rank, own, length)
    outer = jnp.einsum("rsl,qsl->srq", mine[0], mine[1], precision=lax.Precision.HIGHEST)
    sketch = outer.reshape(own, rank * rank) / (length * rank)

    top = lax.reduce_precision(sketch, 8, 7)
    hi, lo = top.astype(BF), (sketch - top).astype(BF)
    rows = jnp.concatenate([hi, lo], 0)
    stacked = jnp.concatenate([rows] + [lax.ppermute(rows, "dp", oshift(k)) for k in range(1, no)], 0)
    far_other = lax.ppermute(far_mine, "tensor", core)

    def score(q):
        s = lax.dot_general(stacked, q, (((1,), (1,)), ((), ())), preferred_element_type=F32)
        s = s.reshape(no, 2, own, -1)
        return s[:, 0] + s[:, 1]

    def back(s):
        return [s[0]] + [lax.ppermute(s[k], "dp", oshift(no - k)) for k in range(1, no)]

    near_s = score(queries)
    fm, fo = score(far_mine), score(far_other)
    far_s = jnp.concatenate([jnp.where(c == 0, fm, fo), jnp.where(c == 0, fo, fm)], 2)
    both = jnp.concatenate([jnp.where(i == 0, near_s, far_s), jnp.where(i == 0, far_s, near_s)], 2)
    allb = jnp.stack(back(both), 0)
    allb = jnp.roll(allb, o, axis=0) if no > 2 else jnp.where(o == 0, allb, allb[::-1])
    return jnp.swapaxes(allb, 0, 1).reshape(own, nd * nq)


def solution(mesh):
    in_specs = (
        P(("groups", "dp"), None, "tensor"),
        P(("groups", "dp"), None, "tensor"),
        P(None, "tensor"),
        P(None, "tensor"),
        P(("groups", "dp"), None),
    )
    out_specs = P(("groups", "dp", "tensor"), None)
    return jax.shard_map(local, mesh=mesh, in_specs=in_specs, out_specs=out_specs, check_vma=False)
```

time: 25.9 us -> 25.7 us (level)
  matrix products: 5.98 us -> 0.85 us
  blocking collectives: 0 us -> 4.94 us
  waiting for transfers between devices: 8.22 us -> 4 us
  local copies, waits for them, and re-layouts: 0.17 us -> 3.41 us
  Pallas kernels: 0 us -> 2.79 us
  starting transfers between devices: 10.4 us -> 8.53 us
    dot_general x3 -> x1, matrix products: 5.37 us -> 0.23 us  [local(): jnp.einsum('rsl,qsl->srq', mine[0], mine[1], precision=lax.Precision.HIGH...]
    all_gather x0 -> x1, blocking collectives: none -> 4.94 us  [local(): everyone = lax.all_gather(sent, 'tensor', axis=0, axis_index_groups=groups)]
    unnamed x6 -> x10, local copies, waits for them, and re-layouts: 0.01 us -> 3.2 us
    ppermute x1, waiting for transfers between devices: 3 us -> 0.01 us  [local(): far_mine = lax.ppermute(part, 'dp', near)]
    pallas_call x0 -> x3, Pallas kernels: none -> 2.79 us  [the longest x2 2.77 us: project(): pl.pallas_call(functools.partial(project_kernel, nx, nt), out_shape=[shap...]
    ppermute x3 -> x2, starting transfers between devices: 5.7 us -> 3.22 us  [the longest x1 2.7 us: back(): lax.ppermute(s[k], 'dp', oshift(no - k))]
    ppermute x3 -> x2, waiting for transfers between devices: 4.12 us -> 1.78 us  [the longest x1 1.78 us: back(): lax.ppermute(s[k], 'dp', oshift(no - k))]
    ppermute x1, waiting for transfers between devices: 0.01 us -> 2.22 us  [local(): lax.ppermute(rows, 'dp', oshift(k))]
  transfers between devices with their start and end apart: 6 -> 5, of which waited for: 5 -> 2; matrix products, arithmetic and copies ran while one was open for 3% -> 4% of each run, Pallas kernels for 0% -> 0%
where the time goes in v2:
time: 25.7 us; the launch traced here: 25.6 us
  starting transfers between devices  8.53 us (33%)
  blocking collectives  4.94 us (19%)
  waiting for transfers between devices  4 us (16%)
  local copies, waits for them, and re-layouts  3.41 us (13%)
  Pallas kernels  2.79 us (11%)
  other arithmetic  0.89 us (3%)
  matrix products  0.85 us (3%)
    all_gather x1, blocking collectives, local(): everyone = lax.all_gather(sent, 'tensor', axis=0, axis_index_groups=groups)  4.94 us
    unnamed x10, local copies, waits for them, and re-layouts  3.2 us
    pallas_call x2, Pallas kernels, project(): pl.pallas_call(functools.partial(project_kernel, nx, nt), out_shape=[shap...  2.77 us
    ppermute x1, starting transfers between devices, back(): lax.ppermute(s[k], 'dp', oshift(no - k))  2.7 us
    ppermute x1, starting transfers between devices, local(): lax.ppermute(rows, 'dp', oshift(k))  2.66 us
    ppermute x1, starting transfers between devices, local(): far_mine = lax.ppermute(part, 'dp', near)  2.65 us
    ppermute x1, waiting for transfers between devices, local(): lax.ppermute(rows, 'dp', oshift(k))  2.22 us
    ppermute x1, waiting for transfers between devices, back(): lax.ppermute(s[k], 'dp', oshift(no - k))  1.78 us
  transfers between devices with their start and end apart: 5, of which 2 were waited for; matrix products, arithmetic and copies ran while one was open for 4% of the time, Pallas kernels for 0%

profile of v2, /device:TPU:0, one launch (start us, length us, event | category | flops | bytes accessed | tf_op | source)
XLA Modules:
  0.0 25.6 jit_solution(14560154103052905762)
XLA Ops:
  0.0 0.0 copy-start
  0.0 1.0 %copy-done = bf16[64,4096]{1,0:T(8,128)(2,1)S(1)} copy-done((bf16[64,4096]{1,0:T(8,128)(2,1)S(1)}, bf16[64,4096]{1,0:T(8,128)(2,1)}, u32[]{:S(2)}) %copy-start) | copy-done | bytes 524312
  1.1 0.0 copy-start.1
  1.1 0.0 copy-start.3
  1.1 0.0 copy-start.2
  1.1 0.0 copy-start.4
  1.1 2.1 %copy-done.1 = bf16[8,128,2048]{2,1,0:T(8,128)(2,1)S(1)} copy-done((bf16[8,128,2048]{2,1,0:T(8,128)(2,1)S(1)}, bf16[8,128,2048]{2,1,0:T(8,128)(2,1)}, u32[]{:S(2)}) %copy-start.1) | copy-done | bytes 4194328
  3.3 0.0 copy-done.3
  3.3 1.4 %shard_map.56 = (f32[2,64,256]{2,1,0:T(8,128)S(1)}, f32[2,64,256]{2,1,0:T(8,128)S(1)}) custom-call(bf16[1024,2048]{1,0:T(8,128)(2,1)S(1)} %bitcast.75, bf16[64,2048]{1,0:T(8,128)(2,1)S(1)} %copy-done.3), custom_call_target="tpu_custom_call" | custom-call | flops 268435456 | bytes 4194304 | tf_op jit(solution)/shard_map/pallas_call | solution.py:45
  4.7 0.0 copy-done.2
  4.7 0.0 copy-done.4
  4.7 1.4 %shard_map.57 = (f32[2,64,256]{2,1,0:T(8,128)S(1)}, f32[2,64,256]{2,1,0:T(8,128)S(1)}) custom-call(bf16[1024,2048]{1,0:T(8,128)(2,1)S(1)} %bitcast.76, bf16[64,2048]{1,0:T(8,128)(2,1)S(1)} %copy-done.4), custom_call_target="tpu_custom_call" | custom-call | flops 268435456 | bytes 4194304 | tf_op jit(solution)/shard_map/pallas_call | solution.py:45
  6.1 0.5 %collective-permute-start = (f32[2,128,256]{2,1,0:T(8,128)S(1)}, f32[2,128,256]{2,1,0:T(8,128)S(1)}, u32[]{:S(2)}, u32[]{:S(2)}) collective-permute-start(f32[2,128,256]{2,1,0:T(8,128)S(1)} %pad_maximum_fusion), channel_id=1, source_target_pairs={{0,1},{1,0},{2,3},{3,2},{4,5},{5,4},{6,7},{7,6},{8,9},{9,8},{10,11... | collective-permute-start | bytes 786440 | tf_op jit(solution)/shard_map/ppermute | solution.py:86
  6.6 2.6 %collective-permute-start.2 = (bf16[32,4096]{1,0:T(8,128)(2,1)S(1)}, bf16[32,4096]{1,0:T(8,128)(2,1)S(1)}, u32[]{:S(2)}, u32[]{:S(2)}) collective-permute-start(bf16[32,4096]{1,0:T(8,128)(2,1)S(1)} %shard_map.55), channel_id=1, source_target_pairs={{0,4},{4,0},{8,12},{12,8},{1,5},{5,1},{9,13},{13,9},{2,6},{6,2},{1... | collective-permute-start | bytes 786440 | tf_op jit(solution)/shard_map/ppermute | solution.py:81
  9.3 0.0 collective-permute-done
  9.3 4.9 %all-gather = bf16[2,128,256]{2,1,0:T(8,128)(2,1)S(1)} all-gather(bf16[1,128,256]{2,1,0:T(8,128)(2,1)S(1)} %slice.117), channel_id=2, replica_groups={{0,2},{1,3},{4,6},{5,7},{8,10},{9,11},{12,14},{13,15},{16,18},{17,19},{..., dimensions={0}, use_global_device_ids=true | all-gather | bytes 196608 | tf_op jit(solution)/shard_map/all_gather | solution.py:91
  14.4 0.2 convolution_multiply_fusion
  14.6 0.1 div.31
  14.8 2.7 %collective-permute-start.1 = (bf16[4,4096]{1,0:T(4,128)(2,1)S(1)}, bf16[4,4096]{1,0:T(4,128)(2,1)S(1)}, u32[]{:S(2)}, u32[]{:S(2)}) collective-permute-start(bf16[4,4096]{1,0:T(4,128)(2,1)S(1)} %pad_maximum_fusion.2), channel_id=1, source_target_pairs={{0,8},{4,12},{8,0},{12,4},{1,9},{5,13},{9,1},{13,5},{2,10},{6,14},... | collective-permute-start | bytes 98312 | tf_op jit(solution)/shard_map/ppermute | solution.py:102
  17.5 0.0 collective-permute-done.2
  17.5 0.0 collective-permute-start.3
  17.5 2.2 %collective-permute-done.1 = bf16[4,4096]{1,0:T(4,128)(2,1)S(1)} collective-permute-done((bf16[4,4096]{1,0:T(4,128)(2,1)S(1)}, bf16[4,4096]{1,0:T(4,128)(2,1)S(1)}, u32[]{:S(2)}, u32[]{:S(2)}) %collective-permute-start.1) | collective-permute-done | bytes 32800 | tf_op jit(solution)/shard_map/ppermute | solution.py:102
  19.7 0.2 fusion.11
  19.9 0.2 fusion.12
  20.1 0.0 collective-permute-done.3
  20.1 0.2 fusion.10
  20.3 0.1 broadcast_select_fusion.1
  20.4 0.1 fusion.8
  20.5 2.7 %collective-permute-start.4 = (f32[2,128]{1,0:T(2,128)S(1)}, f32[2,128]{1,0:T(2,128)S(1)}, u32[]{:S(2)}, u32[]{:S(2)}) collective-permute-start(f32[2,128]{1,0:T(2,128)S(1)} %get-tuple-element.26), channel_id=1, source_target_pairs={{0,8},{4,12},{8,0},{12,4},{1,9},{5,13},{9,1},{13,5},{2,10},{6,14},... | collective-permute-start | bytes 3080 | tf_op jit(solution)/shard_map/ppermute | solution.py:111
  23.2 1.8 %collective-permute-done.4 = f32[2,128]{1,0:T(2,128)S(1)} collective-permute-done((f32[2,128]{1,0:T(2,128)S(1)}, f32[2,128]{1,0:T(2,128)S(1)}, u32[]{:S(2)}, u32[]{:S(2)}) %collective-permute-start.4) | collective-permute-done | bytes 1056 | tf_op jit(solution)/shard_map/ppermute | solution.py:111
  25.0 0.6 %fusion.3 = f32[2,256]{1,0:T(2,128)} fusion(f32[2,2,128]{2,1,0:T(2,128)S(1)} %pad_maximum_fusion.4, pred[]{:T(512)S(6)} %eq.15), kind=kLoop, calls=%fused_computation.13 | loop fusion | flops 512 | bytes 4097 | tf_op jit(solution)/shard_map/reshape | solution.py:119
  (13 shorter events, 0.3 us)
Async XLA Ops:
  0.0 1.0 %copy-start = (bf16[64,4096]{1,0:T(8,128)(2,1)S(1)}, bf16[64,4096]{1,0:T(8,128)(2,1)}, u32[]{:S(2)}) copy-start(bf16[64,4096]{1,0:T(8,128)(2,1)} %param.9) | copy-start | bytes 1572868
  1.1 2.2 %copy-start.1 = (bf16[8,128,2048]{2,1,0:T(8,128)(2,1)S(1)}, bf16[8,128,2048]{2,1,0:T(8,128)(2,1)}, u32[]{:S(2)}) copy-start(bf16[8,128,2048]{2,1,0:T(8,128)(2,1)} %param.5) | copy-start | bytes 12582916
  1.1 2.2 %copy-start.3 = (bf16[64,2048]{1,0:T(8,128)(2,1)S(1)}, bf16[64,2048]{1,0:T(8,128)(2,1)}, u32[]{:S(2)}) copy-start(bf16[64,2048]{1,0:T(8,128)(2,1)} %basis.2) | copy-start | bytes 786436
  1.1 3.5 %copy-start.2 = (bf16[8,128,2048]{2,1,0:T(8,128)(2,1)S(1)}, bf16[8,128,2048]{2,1,0:T(8,128)(2,1)}, u32[]{:S(2)}) copy-start(bf16[8,128,2048]{2,1,0:T(8,128)(2,1)} %param.6) | copy-start | bytes 12582916
  1.1 3.5 %copy-start.4 = (bf16[64,2048]{1,0:T(8,128)(2,1)S(1)}, bf16[64,2048]{1,0:T(8,128)(2,1)}, u32[]{:S(2)}) copy-start(bf16[64,2048]{1,0:T(8,128)(2,1)} %basis.3) | copy-start | bytes 786436
  6.1 3.2 %collective-permute-start = (f32[2,128,256]{2,1,0:T(8,128)S(1)}, f32[2,128,256]{2,1,0:T(8,128)S(1)}, u32[]{:S(2)}, u32[]{:S(2)}) collective-permute-start(f32[2,128,256]{2,1,0:T(8,128)S(1)} %pad_maximum_fusion), channel_id=1, source_target_pairs={{0,1},{1,0},{2,3},{3,2},{4,5},{5,4},{6,7},{7,6},{8,9},{9,8},{10,11... | collective-permute-start | bytes 786440 | tf_op jit(solution)/shard_map/ppermute | solution.py:86
  6.6 10.9 %collective-permute-start.2 = (bf16[32,4096]{1,0:T(8,128)(2,1)S(1)}, bf16[32,4096]{1,0:T(8,128)(2,1)S(1)}, u32[]{:S(2)}, u32[]{:S(2)}) collective-permute-start(bf16[32,4096]{1,0:T(8,128)(2,1)S(1)} %shard_map.55), channel_id=1, source_target_pairs={{0,4},{4,0},{8,12},{12,8},{1,5},{5,1},{9,13},{13,9},{2,6},{6,2},{1... | collective-permute-start | bytes 786440 | tf_op jit(solution)/shard_map/ppermute | solution.py:81
  14.8 4.9 %collective-permute-start.1 = (bf16[4,4096]{1,0:T(4,128)(2,1)S(1)}, bf16[4,4096]{1,0:T(4,128)(2,1)S(1)}, u32[]{:S(2)}, u32[]{:S(2)}) collective-permute-start(bf16[4,4096]{1,0:T(4,128)(2,1)S(1)} %pad_maximum_fusion.2), channel_id=1, source_target_pairs={{0,8},{4,12},{8,0},{12,4},{1,9},{5,13},{9,1},{13,5},{2,10},{6,14},... | collective-permute-start | bytes 98312 | tf_op jit(solution)/shard_map/ppermute | solution.py:102
  17.5 2.6 %collective-permute-start.3 = (bf16[32,4096]{1,0:T(8,128)(2,1)S(1)}, bf16[32,4096]{1,0:T(8,128)(2,1)S(1)}, u32[]{:S(2)}, u32[]{:S(2)}) collective-permute-start(bf16[32,4096]{1,0:T(8,128)(2,1)S(1)} %collective-permute-done.2), channel_id=1, source_target_pairs={{0,1},{1,0},{2,3},{3,2},{4,5},{5,4},{6,7},{7,6},{8,9},{9,8},{10,11... | collective-permute-start | bytes 786440 | tf_op jit(solution)/shard_map/ppermute | solution.py:103
  20.5 4.5 %collective-permute-start.4 = (f32[2,128]{1,0:T(2,128)S(1)}, f32[2,128]{1,0:T(2,128)S(1)}, u32[]{:S(2)}, u32[]{:S(2)}) collective-permute-start(f32[2,128]{1,0:T(2,128)S(1)} %get-tuple-element.26), channel_id=1, source_target_pairs={{0,8},{4,12},{8,0},{12,4},{1,9},{5,13},{9,1},{13,5},{2,10},{6,14},... | collective-permute-start | bytes 3080 | tf_op jit(solution)/shard_map/ppermute | solution.py:111

commit v3 on v2

--- a/solution.py
+++ b/solution.py
@@ -10,22 +10,21 @@
 BF, F32 = jnp.bfloat16, jnp.float32
 
 
-def settle_kernel(arrived, held):
-    held[...] = arrived[...]
+def open_kernel(token):
+    token[...] = jnp.zeros_like(token)
 
 
-def settle(arrived):
+def opening():
     return pl.pallas_call(
-        settle_kernel,
-        out_shape=jax.ShapeDtypeStruct(arrived.shape, arrived.dtype),
-        in_specs=[pl.BlockSpec(memory_space=pltpu.VMEM)],
+        open_kernel,
+        out_shape=jax.ShapeDtypeStruct((8, 128), F32),
         out_specs=pl.BlockSpec(memory_space=pltpu.VMEM),
         compiler_params=pltpu.CompilerParams(vmem_limit_bytes=16 * 2**20),
         cost_estimate=pl.CostEstimate(flops=10000000000, bytes_accessed=0, transcendentals=0),
-    )(arrived)
+    )()
 
 
-def project_kernel(nx, nt, values, basis, give, keep):
+def project_kernel(nx, nt, values, basis, token, give, keep):
     rows = give.shape[2]
     t = lax.axis_index("tensor")
     x, c = t // 2, t % 2
@@ -37,7 +36,7 @@
         to[k] = lax.dot_general(basis[...], values[source], (((1,), (1,)), ((), ())), preferred_element_type=F32)
 
 
-def project(values, basis, nt):
+def project(values, basis, token, nt):
     rank, hidden = basis.shape
     rows = values.shape[0] // nt
     nx = nt // 2
@@ -45,11 +44,38 @@
     return pl.pallas_call(
         functools.partial(project_kernel, nx, nt),
         out_shape=[shape, shape],
-        in_specs=[pl.BlockSpec(memory_space=pltpu.VMEM)] * 2,
+        in_specs=[pl.BlockSpec(memory_space=pltpu.VMEM)] * 3,
         out_specs=[pl.BlockSpec(memory_space=pltpu.VMEM)] * 2,
         compiler_params=pltpu.CompilerParams(vmem_limit_bytes=16 * 2**20),
         cost_estimate=pl.CostEstimate(flops=2 * nt * rows * hidden * rank, bytes_accessed=2 * nt * rows * hidden, transcendentals=0),
-    )(values, basis)
+    )(values, basis, token)
+
+
+def score_kernel(no, own, outer_axis, rows, near, mine, other, out):
+    c = lax.axis_index("tensor") % 2
+    d = lax.axis_index("dp")
+    i = d % 2 if outer_axis else d // no
+
+    def product(q):
+        return lax.dot_general(rows[...], q[...], (((1,), (1,)), ((), ())), preferred_element_type=F32)
+
+    n, m, f = product(near), product(mine), product(other)
+    far = jnp.where(c == 0, jnp.concatenate([m, f], 1), jnp.concatenate([f, m], 1))
+    every = jnp.where(i == 0, jnp.concatenate([n, far], 1), jnp.concatenate([far, n], 1))
+    for k in range(no):
+        at = 2 * own * k
+        out[k] = every[at : at + own] + every[at + own : at + 2 * own]
+
+
+def score(rows, near, mine, other, no, own, outer_axis):
+    return pl.pallas_call(
+        functools.partial(score_kernel, no, own, outer_axis),
+        out_shape=jax.ShapeDtypeStruct((no, own, 2 * near.shape[0]), F32),
+        in_specs=[pl.BlockSpec(memory_space=pltpu.VMEM)] * 4,
+        out_specs=pl.BlockSpec(memory_space=pltpu.VMEM),
+        compiler_params=pltpu.CompilerParams(vmem_limit_bytes=16 * 2**20),
+        cost_estimate=pl.CostEstimate(flops=4 * rows.size * near.shape[0], bytes_accessed=2 * near.size, transcendentals=0),
+    )(rows, near, mine, other)
 
 
 def local(acts, grads, basis_in, basis_out, queries):
@@ -77,12 +103,12 @@
     near = [(at(a, b), at(a, 1 - b)) for a in range(no) for b in range(2)]
 
     half, depth = nq // 2, queries.shape[1]
-    part = settle(lax.dynamic_slice_in_dim(queries, c * half, half, 0))
+    part = lax.dynamic_slice_in_dim(queries, c * half, half, 0)
+    token = opening()
     far_mine = lax.ppermute(part, "dp", near)
-    acts, grads, part = lax.optimization_barrier((acts, grads, part))
 
-    give_r, keep_r = project(grads.reshape(-1, hidden), basis_out, nt)
-    give_l, keep_l = project(acts.reshape(-1, hidden), basis_in, nt)
+    give_r, keep_r = project(grads.reshape(-1, hidden), basis_out, token, nt)
+    give_l, keep_l = project(acts.reshape(-1, hidden), basis_in, token, nt)
     got = lax.ppermute(jnp.concatenate([give_l, give_r], 1), "tensor", core)
     keep = jnp.concatenate([keep_l, keep_r], 1) + got
     mine = keep[0]
@@ -102,19 +128,10 @@
     stacked = jnp.concatenate([rows] + [lax.ppermute(rows, "dp", oshift(k)) for k in range(1, no)], 0)
     far_other = lax.ppermute(far_mine, "tensor", core)
 
-    def score(q):
-        s = lax.dot_general(stacked, q, (((1,), (1,)), ((), ())), preferred_element_type=F32)
-        s = s.reshape(no, 2, own, -1)
-        return s[:, 0] + s[:, 1]
-
     def back(s):
         return [s[0]] + [lax.ppermute(s[k], "dp", oshift(no - k)) for k in range(1, no)]
 
-    near_s = score(queries)
-    fm, fo = score(far_mine), score(far_other)
-    far_s = jnp.concatenate([jnp.where(c == 0, fm, fo), jnp.where(c == 0, fo, fm)], 2)
-    both = jnp.concatenate([jnp.where(i == 0, near_s, far_s), jnp.where(i == 0, far_s, near_s)], 2)
-    allb = jnp.stack(back(both), 0)
+    allb = jnp.stack(back(score(stacked, queries, far_mine, far_other, no, own, True)), 0)
     allb = jnp.roll(allb, o, axis=0) if no > 2 else jnp.where(o == 0, allb, allb[::-1])
     return jnp.swapaxes(allb, 0, 1).reshape(own, nd * nq)
 

time: 25.7 us -> 24.5 us (0.953)
  local copies, waits for them, and re-layouts: 3.41 us -> 2.43 us
  matrix products: 0.85 us -> 0.23 us
  Pallas kernels: 2.79 us -> 3.23 us
    unnamed x10, local copies, waits for them, and re-layouts: 3.2 us -> 2.21 us
    dot_general x3 -> x0, matrix products: 0.62 us -> none  [score(): lax.dot_general(stacked, q, (((1,), (1,)), ((), ())), preferred_element_t...]
    pallas_call x1 -> x2, Pallas kernels: 0.02 us -> 0.45 us  [the longest x1 0.45 us: score(): pl.pallas_call(functools.partial(score_kernel, no, own, outer_axis), out_...]
  transfers between devices with their start and end apart: 5 -> 5, of which waited for: 2 -> 2; matrix products, arithmetic and copies ran while one was open for 4% -> 3% of each run, Pallas kernels for 0% -> 0%
where the time goes in v3:
time: 24.5 us; the launch traced here: 24.4 us
  starting transfers between devices  8.62 us (35%)
  blocking collectives  4.94 us (20%)
  waiting for transfers between devices  4 us (16%)
  Pallas kernels  3.23 us (13%)
  local copies, waits for them, and re-layouts  2.43 us (10%)
  other arithmetic  0.78 us (3%)
    all_gather x1, blocking collectives, local(): everyone = lax.all_gather(sent, 'tensor', axis=0, axis_index_groups=groups)  4.94 us
    pallas_call x2, Pallas kernels, project(): pl.pallas_call(functools.partial(project_kernel, nx, nt), out_shape=[shap...  2.77 us
    ppermute x1, starting transfers between devices, back(): lax.ppermute(s[k], 'dp', oshift(no - k))  2.76 us
    ppermute x1, starting transfers between devices, local(): far_mine = lax.ppermute(part, 'dp', near)  2.68 us
    ppermute x1, starting transfers between devices, local(): lax.ppermute(rows, 'dp', oshift(k))  2.66 us
    ppermute x1, waiting for transfers between devices, local(): lax.ppermute(rows, 'dp', oshift(k))  2.22 us
    unnamed x10, local copies, waits for them, and re-layouts  2.21 us
    ppermute x1, waiting for transfers between devices, back(): lax.ppermute(s[k], 'dp', oshift(no - k))  1.78 us
  transfers between devices with their start and end apart: 5, of which 2 were waited for; matrix products, arithmetic and copies ran while one was open for 3% of the time, Pallas kernels for 0%

profile of v3, /device:TPU:0, one launch (start us, length us, event | category | flops | bytes accessed | tf_op | source)
XLA Modules:
  0.0 24.4 jit_solution(17190257983272058109)
XLA Ops:
  0.0 0.0 copy-start
  0.0 0.0 copy-start.3
  0.0 0.0 copy-start.1
  0.0 0.0 copy-start.4
  0.0 2.2 %copy-done = bf16[8,128,2048]{2,1,0:T(8,128)(2,1)S(1)} copy-done((bf16[8,128,2048]{2,1,0:T(8,128)(2,1)S(1)}, bf16[8,128,2048]{2,1,0:T(8,128)(2,1)}, u32[]{:S(2)}) %copy-start) | copy-done | bytes 4194328
  2.2 0.0 copy-done.3
  2.2 0.0 copy-start.2
  2.2 1.4 %shard_map.57 = (f32[2,64,256]{2,1,0:T(8,128)S(1)}, f32[2,64,256]{2,1,0:T(8,128)S(1)}) custom-call(bf16[1024,2048]{1,0:T(8,128)(2,1)S(1)} %bitcast.9, bf16[64,2048]{1,0:T(8,128)(2,1)S(1)} %copy-done.3, f32[8,128]{1,0:T(8,128)S(1)} %shard_map.55.token), custom_call_target="tpu_custom_call" | custom-call | flops 268435456 | bytes 4194304 | tf_op jit(solution)/shard_map/pallas_call | solution.py:44
  3.6 0.0 copy-done.1
  3.6 0.0 copy-done.4
  3.6 1.4 %shard_map.56 = (f32[2,64,256]{2,1,0:T(8,128)S(1)}, f32[2,64,256]{2,1,0:T(8,128)S(1)}) custom-call(bf16[1024,2048]{1,0:T(8,128)(2,1)S(1)} %bitcast.10, bf16[64,2048]{1,0:T(8,128)(2,1)S(1)} %copy-done.4, f32[8,128]{1,0:T(8,128)S(1)} %shard_map.55.token), custom_call_target="tpu_custom_call" | custom-call | flops 268435456 | bytes 4194304 | tf_op jit(solution)/shard_map/pallas_call | solution.py:44
  5.0 0.5 %collective-permute-start = (f32[2,128,256]{2,1,0:T(8,128)S(1)}, f32[2,128,256]{2,1,0:T(8,128)S(1)}, u32[]{:S(2)}, u32[]{:S(2)}) collective-permute-start(f32[2,128,256]{2,1,0:T(8,128)S(1)} %pad_maximum_fusion), channel_id=1, source_target_pairs={{0,1},{1,0},{2,3},{3,2},{4,5},{5,4},{6,7},{7,6},{8,9},{9,8},{10,11... | collective-permute-start | bytes 786440 | tf_op jit(solution)/shard_map/ppermute | solution.py:112
  5.6 0.0 copy-done.2
  5.6 2.7 %collective-permute-start.2 = (bf16[32,4096]{1,0:T(8,128)(2,1)S(1)}, bf16[32,4096]{1,0:T(8,128)(2,1)S(1)}, u32[]{:S(2)}, u32[]{:S(2)}) collective-permute-start(bf16[32,4096]{1,0:T(8,128)(2,1)S(1)} %constant_dynamic-slice_fusion), channel_id=1, source_target_pairs={{0,4},{4,0},{8,12},{12,8},{1,5},{5,1},{9,13},{13,9},{2,6},{6,2},{1... | collective-permute-start | bytes 786440 | tf_op jit(solution)/shard_map/ppermute | solution.py:108
  8.3 0.0 collective-permute-done
  8.3 4.9 %all-gather = bf16[2,128,256]{2,1,0:T(8,128)(2,1)S(1)} all-gather(bf16[1,128,256]{2,1,0:T(8,128)(2,1)S(1)} %slice.38), channel_id=2, replica_groups={{0,2},{1,3},{4,6},{5,7},{8,10},{9,11},{12,14},{13,15},{16,18},{17,19},{..., dimensions={0}, use_global_device_ids=true | all-gather | bytes 196608 | tf_op jit(solution)/shard_map/all_gather | solution.py:117
  13.4 0.2 convolution_multiply_fusion
  13.6 0.1 div.31
  13.8 2.7 %collective-permute-start.1 = (bf16[4,4096]{1,0:T(4,128)(2,1)S(1)}, bf16[4,4096]{1,0:T(4,128)(2,1)S(1)}, u32[]{:S(2)}, u32[]{:S(2)}) collective-permute-start(bf16[4,4096]{1,0:T(4,128)(2,1)S(1)} %pad_maximum_fusion.2), channel_id=1, source_target_pairs={{0,8},{4,12},{8,0},{12,4},{1,9},{5,13},{9,1},{13,5},{2,10},{6,14},... | collective-permute-start | bytes 98312 | tf_op jit(solution)/shard_map/ppermute | solution.py:128
  16.5 0.0 collective-permute-done.2.mine
  16.5 0.0 collective-permute-start.3
  16.5 2.2 %collective-permute-done.1 = bf16[4,4096]{1,0:T(4,128)(2,1)S(1)} collective-permute-done((bf16[4,4096]{1,0:T(4,128)(2,1)S(1)}, bf16[4,4096]{1,0:T(4,128)(2,1)S(1)}, u32[]{:S(2)}, u32[]{:S(2)}) %collective-permute-start.1) | collective-permute-done | bytes 32800 | tf_op jit(solution)/shard_map/ppermute | solution.py:128
  18.7 0.1 pad_maximum_fusion.1.rows
  18.8 0.0 collective-permute-done.3.other
  18.8 0.4 %shard_map.58 = f32[2,2,128]{2,1,0:T(2,128)S(1)} custom-call(bf16[8,4096]{1,0:T(8,128)(2,1)S(1)} %pad_maximum_fusion.1.rows, bf16[64,4096]{1,0:T(8,128)(2,1)S(1)} %copy-done.2, bf16[32,4096]{1,0:T(8,128)(2,1)S(1)} %collective-permute-done.2.mine, bf16[32,4096]{1,0:T(8,128)(2,1)S(1)} %collective-permute-done.3.other), custom_call_target="tpu_custom_call" | custom-call | flops 8388608 | bytes 524288 | tf_op jit(solution)/shard_map/pallas_call | solution.py:71
  19.2 2.8 %collective-permute-start.4 = (f32[2,128]{1,0:T(2,128)S(1)}, f32[2,128]{1,0:T(2,128)S(1)}, u32[]{:S(2)}, u32[]{:S(2)}) collective-permute-start(f32[2,128]{1,0:T(2,128)S(1)} %get-tuple-element.18), channel_id=1, source_target_pairs={{0,8},{4,12},{8,0},{12,4},{1,9},{5,13},{9,1},{13,5},{2,10},{6,14},... | collective-permute-start | bytes 3080 | tf_op jit(solution)/shard_map/ppermute | solution.py:132
  22.0 1.8 %collective-permute-done.4 = f32[2,128]{1,0:T(2,128)S(1)} collective-permute-done((f32[2,128]{1,0:T(2,128)S(1)}, f32[2,128]{1,0:T(2,128)S(1)}, u32[]{:S(2)}, u32[]{:S(2)}) %collective-permute-start.4) | collective-permute-done | bytes 1056 | tf_op jit(solution)/shard_map/ppermute | solution.py:132
  23.8 0.6 %fusion.3 = f32[2,256]{1,0:T(2,128)} fusion(f32[2,2,128]{2,1,0:T(2,128)S(1)} %pad_maximum_fusion.3, pred[]{:T(512)S(6)} %eq.6), kind=kLoop, calls=%fused_computation.13 | loop fusion | flops 512 | bytes 4097 | tf_op jit(solution)/shard_map/reshape | solution.py:136
  (13 shorter events, 0.3 us)
Async XLA Ops:
  0.0 2.2 %copy-start = (bf16[8,128,2048]{2,1,0:T(8,128)(2,1)S(1)}, bf16[8,128,2048]{2,1,0:T(8,128)(2,1)}, u32[]{:S(2)}) copy-start(bf16[8,128,2048]{2,1,0:T(8,128)(2,1)} %param.6) | copy-start | bytes 12582916
  0.0 2.2 %copy-start.3 = (bf16[64,2048]{1,0:T(8,128)(2,1)S(1)}, bf16[64,2048]{1,0:T(8,128)(2,1)}, u32[]{:S(2)}) copy-start(bf16[64,2048]{1,0:T(8,128)(2,1)} %basis.3) | copy-start | bytes 786436
  0.0 3.6 %copy-start.1 = (bf16[8,128,2048]{2,1,0:T(8,128)(2,1)S(1)}, bf16[8,128,2048]{2,1,0:T(8,128)(2,1)}, u32[]{:S(2)}) copy-start(bf16[8,128,2048]{2,1,0:T(8,128)(2,1)} %param.5) | copy-start | bytes 12582916
  0.0 3.6 %copy-start.4 = (bf16[64,2048]{1,0:T(8,128)(2,1)S(1)}, bf16[64,2048]{1,0:T(8,128)(2,1)}, u32[]{:S(2)}) copy-start(bf16[64,2048]{1,0:T(8,128)(2,1)} %basis.2) | copy-start | bytes 786436
  2.2 3.4 %copy-start.2 = (bf16[64,4096]{1,0:T(8,128)(2,1)S(1)}, bf16[64,4096]{1,0:T(8,128)(2,1)}, u32[]{:S(2)}) copy-start(bf16[64,4096]{1,0:T(8,128)(2,1)} %near.1) | copy-start | bytes 1572868
  5.0 3.2 %collective-permute-start = (f32[2,128,256]{2,1,0:T(8,128)S(1)}, f32[2,128,256]{2,1,0:T(8,128)S(1)}, u32[]{:S(2)}, u32[]{:S(2)}) collective-permute-start(f32[2,128,256]{2,1,0:T(8,128)S(1)} %pad_maximum_fusion), channel_id=1, source_target_pairs={{0,1},{1,0},{2,3},{3,2},{4,5},{5,4},{6,7},{7,6},{8,9},{9,8},{10,11... | collective-permute-start | bytes 786440 | tf_op jit(solution)/shard_map/ppermute | solution.py:112
  5.6 10.9 %collective-permute-start.2 = (bf16[32,4096]{1,0:T(8,128)(2,1)S(1)}, bf16[32,4096]{1,0:T(8,128)(2,1)S(1)}, u32[]{:S(2)}, u32[]{:S(2)}) collective-permute-start(bf16[32,4096]{1,0:T(8,128)(2,1)S(1)} %constant_dynamic-slice_fusion), channel_id=1, source_target_pairs={{0,4},{4,0},{8,12},{12,8},{1,5},{5,1},{9,13},{13,9},{2,6},{6,2},{1... | collective-permute-start | bytes 786440 | tf_op jit(solution)/shard_map/ppermute | solution.py:108
  13.8 4.9 %collective-permute-start.1 = (bf16[4,4096]{1,0:T(4,128)(2,1)S(1)}, bf16[4,4096]{1,0:T(4,128)(2,1)S(1)}, u32[]{:S(2)}, u32[]{:S(2)}) collective-permute-start(bf16[4,4096]{1,0:T(4,128)(2,1)S(1)} %pad_maximum_fusion.2), channel_id=1, source_target_pairs={{0,8},{4,12},{8,0},{12,4},{1,9},{5,13},{9,1},{13,5},{2,10},{6,14},... | collective-permute-start | bytes 98312 | tf_op jit(solution)/shard_map/ppermute | solution.py:128
  16.5 2.3 %collective-permute-start.3 = (bf16[32,4096]{1,0:T(8,128)(2,1)S(1)}, bf16[32,4096]{1,0:T(8,128)(2,1)S(1)}, u32[]{:S(2)}, u32[]{:S(2)}) collective-permute-start(bf16[32,4096]{1,0:T(8,128)(2,1)S(1)} %collective-permute-done.2.mine), channel_id=1, source_target_pairs={{0,1},{1,0},{2,3},{3,2},{4,5},{5,4},{6,7},{7,6},{8,9},{9,8},{10,11... | collective-permute-start | bytes 786440 | tf_op jit(solution)/shard_map/ppermute | solution.py:129
  19.2 4.5 %collective-permute-start.4 = (f32[2,128]{1,0:T(2,128)S(1)}, f32[2,128]{1,0:T(2,128)S(1)}, u32[]{:S(2)}, u32[]{:S(2)}) collective-permute-start(f32[2,128]{1,0:T(2,128)S(1)} %get-tuple-element.18), channel_id=1, source_target_pairs={{0,8},{4,12},{8,0},{12,4},{1,9},{5,13},{9,1},{13,5},{2,10},{6,14},... | collective-permute-start | bytes 3080 | tf_op jit(solution)/shard_map/ppermute | solution.py:132

commit v4 on v3

--- a/solution.py
+++ b/solution.py
@@ -33,7 +33,7 @@
         place = lax.rem(x + k, nx) * 2 + ((1 - c) if other else c)
         source = pl.ds(pl.multiple_of(place * rows, rows), rows)
         to = give if other else keep
-        to[k] = lax.dot_general(basis[...], values[source], (((1,), (1,)), ((), ())), preferred_element_type=F32)
+        to[k] = lax.dot_general(values[source], basis[...], (((1,), (1,)), ((), ())), preferred_element_type=F32).T
 
 
 def project(values, basis, token, nt):
@@ -51,20 +51,48 @@
     )(values, basis, token)
 
 
+def outer_kernel(nx, own, scale, keep, everyone, sketch):
+    x = lax.axis_index("tensor") // 2
+    mine = keep[0]
+    for k in range(1, nx):
+        mine = mine + everyone[lax.rem(x + nx - k, nx), k - 1].astype(F32)
+    rank, length = mine.shape[0] // 2, mine.shape[1] // own
+    for s in range(own):
+        part = mine[:, s * length : (s + 1) * length]
+        sketch[s] = scale * lax.dot_general(
+            part[:rank], part[rank:], (((1,), (1,)), ((), ())), precision=lax.Precision.HIGHEST, preferred_element_type=F32
+        )
+
+
+def outer(keep, everyone, own):
+    nx, twice, tokens = keep.shape
+    rank = twice // 2
+    return pl.pallas_call(
+        functools.partial(outer_kernel, nx, own, 1.0 / (tokens // own * rank)),
+        out_shape=jax.ShapeDtypeStruct((own, rank, rank), F32),
+        in_specs=[pl.BlockSpec(memory_space=pltpu.VMEM)] * 2,
+        out_specs=pl.BlockSpec(memory_space=pltpu.VMEM),
+        compiler_params=pltpu.CompilerParams(vmem_limit_bytes=16 * 2**20),
+        cost_estimate=pl.CostEstimate(flops=12 * rank * rank * tokens, bytes_accessed=4 * keep.size, transcendentals=0),
+    )(keep, everyone)
+
+
 def score_kernel(no, own, outer_axis, rows, near, mine, other, out):
     c = lax.axis_index("tensor") % 2
+    value = rows[...]
+    hi = value.astype(BF).astype(F32)
+    split = jnp.concatenate([hi, value - hi], 0).astype(BF)
     d = lax.axis_index("dp")
     i = d % 2 if outer_axis else d // no
 
     def product(q):
-        return lax.dot_general(rows[...], q[...], (((1,), (1,)), ((), ())), preferred_element_type=F32)
+        return lax.dot_general(split, q[...], (((1,), (1,)), ((), ())), preferred_element_type=F32)
 
     n, m, f = product(near), product(mine), product(other)
     far = jnp.where(c == 0, jnp.concatenate([m, f], 1), jnp.concatenate([f, m], 1))
     every = jnp.where(i == 0, jnp.concatenate([n, far], 1), jnp.concatenate([far, n], 1))
     for k in range(no):
-        at = 2 * own * k
-        out[k] = every[at : at + own] + every[at + own : at + 2 * own]
+        out[k] = every[own * k : own * (k + 1)] + every[own * (no + k) : own * (no + k + 1)]
 
 
 def score(rows, near, mine, other, no, own, outer_axis):
@@ -74,7 +102,7 @@
         in_specs=[pl.BlockSpec(memory_space=pltpu.VMEM)] * 4,
         out_specs=pl.BlockSpec(memory_space=pltpu.VMEM),
         compiler_params=pltpu.CompilerParams(vmem_limit_bytes=16 * 2**20),
-        cost_estimate=pl.CostEstimate(flops=4 * rows.size * near.shape[0], bytes_accessed=2 * near.size, transcendentals=0),
+        cost_estimate=pl.CostEstimate(flops=8 * rows.size * near.shape[0], bytes_accessed=2 * near.size, transcendentals=0),
     )(rows, near, mine, other)
 
 
@@ -111,20 +139,10 @@
     give_l, keep_l = project(acts.reshape(-1, hidden), basis_in, token, nt)
     got = lax.ppermute(jnp.concatenate([give_l, give_r], 1), "tensor", core)
     keep = jnp.concatenate([keep_l, keep_r], 1) + got
-    mine = keep[0]
-    groups = [[a * 2 + b for a in range(nx)] for b in range(2)]
+    columns = [[a * 2 + b for a in range(nx)] for b in range(2)]
     sent = jnp.stack([keep[k] for k in range(1, nx)], 0).astype(BF)
-    everyone = lax.all_gather(sent, "tensor", axis=0, axis_index_groups=groups)
-    x = t // 2
-    for k in range(1, nx):
-        mine = mine + lax.dynamic_index_in_dim(everyone, (x - k) % nx, 0, False)[k - 1].astype(F32)
-    mine = mine.reshape(2, rank, own, length)
-    outer = jnp.einsum("rsl,qsl->srq", mine[0], mine[1], precision=lax.Precision.HIGHEST)
-    sketch = outer.reshape(own, rank * rank) / (length * rank)
-
-    top = lax.reduce_precision(sketch, 8, 7)
-    hi, lo = top.astype(BF), (sketch - top).astype(BF)
-    rows = jnp.concatenate([hi, lo], 0)
+    everyone = lax.all_gather(sent, "tensor", axis=0, axis_index_groups=columns)
+    rows = outer(keep, everyone, own).reshape(own, rank * rank)
     stacked = jnp.concatenate([rows] + [lax.ppermute(rows, "dp", oshift(k)) for k in range(1, no)], 0)
     far_other = lax.ppermute(far_mine, "tensor", core)
 

time: 24.5 us -> 24.1 us (0.984)
  transfers between devices with their start and end apart: 5 -> 5, of which waited for: 2 -> 2; matrix products, arithmetic and copies ran while one was open for 3% -> 1% of each run, Pallas kernels for 0% -> 1%
where the time goes in v4:
time: 24.1 us; the launch traced here: 24 us
  starting transfers between devices  8.62 us (36%)
  blocking collectives  4.94 us (20%)
  waiting for transfers between devices  4 us (17%)
  Pallas kernels  3.26 us (14%)
  local copies, waits for them, and re-layouts  2.39 us (10%)
  other arithmetic  0.68 us (3%)
    all_gather x1, blocking collectives, local(): everyone = lax.all_gather(sent, 'tensor', axis=0, axis_index_groups=columns)  4.94 us
    ppermute x1, starting transfers between devices, back(): lax.ppermute(s[k], 'dp', oshift(no - k))  2.76 us
    ppermute x1, starting transfers between devices, local(): far_mine = lax.ppermute(part, 'dp', near)  2.68 us
    ppermute x1, starting transfers between devices, local(): lax.ppermute(rows, 'dp', oshift(k))  2.66 us
    pallas_call x2, Pallas kernels, project(): pl.pallas_call(functools.partial(project_kernel, nx, nt), out_shape=[shap...  2.6 us
    unnamed x10, local copies, waits for them, and re-layouts  2.24 us
    ppermute x1, waiting for transfers between devices, local(): lax.ppermute(rows, 'dp', oshift(k))  2.22 us
    ppermute x1, waiting for transfers between devices, back(): lax.ppermute(s[k], 'dp', oshift(no - k))  1.78 us
  transfers between devices with their start and end apart: 5, of which 2 were waited for; matrix products, arithmetic and copies ran while one was open for 1% of the time, Pallas kernels for 1%

profile of v4, /device:TPU:0, one launch (start us, length us, event | category | flops | bytes accessed | tf_op | source)
XLA Modules:
  0.0 24.0 jit_solution(16244431583626603488)
XLA Ops:
  0.0 0.0 copy-start
  0.0 0.0 copy-start.3
  0.0 0.0 copy-start.1
  0.0 0.0 copy-start.4
  0.0 2.2 %copy-done = bf16[8,128,2048]{2,1,0:T(8,128)(2,1)S(1)} copy-done((bf16[8,128,2048]{2,1,0:T(8,128)(2,1)S(1)}, bf16[8,128,2048]{2,1,0:T(8,128)(2,1)}, u32[]{:S(2)}) %copy-start) | copy-done | bytes 4194328
  2.2 0.0 copy-done.3
  2.2 0.0 copy-start.2
  2.2 1.3 %shard_map.57 = (f32[2,64,256]{2,1,0:T(8,128)S(1)}, f32[2,64,256]{2,1,0:T(8,128)S(1)}) custom-call(bf16[1024,2048]{1,0:T(8,128)(2,1)S(1)} %bitcast.10, bf16[64,2048]{1,0:T(8,128)(2,1)S(1)} %copy-done.3, f32[8,128]{1,0:T(8,128)S(1)} %shard_map.55.token), custom_call_target="tpu_custom_call" | custom-call | flops 268435456 | bytes 4194304 | tf_op jit(solution)/shard_map/pallas_call | solution.py:44
  3.5 0.0 copy-done.1
  3.5 0.0 copy-done.4
  3.5 1.3 %shard_map.56 = (f32[2,64,256]{2,1,0:T(8,128)S(1)}, f32[2,64,256]{2,1,0:T(8,128)S(1)}) custom-call(bf16[1024,2048]{1,0:T(8,128)(2,1)S(1)} %bitcast.11, bf16[64,2048]{1,0:T(8,128)(2,1)S(1)} %copy-done.4, f32[8,128]{1,0:T(8,128)S(1)} %shard_map.55.token), custom_call_target="tpu_custom_call" | custom-call | flops 268435456 | bytes 4194304 | tf_op jit(solution)/shard_map/pallas_call | solution.py:44
  4.9 0.5 %collective-permute-start = (f32[2,128,256]{2,1,0:T(8,128)S(1)}, f32[2,128,256]{2,1,0:T(8,128)S(1)}, u32[]{:S(2)}, u32[]{:S(2)}) collective-permute-start(f32[2,128,256]{2,1,0:T(8,128)S(1)} %pad_maximum_fusion), channel_id=1, source_target_pairs={{0,1},{1,0},{2,3},{3,2},{4,5},{5,4},{6,7},{7,6},{8,9},{9,8},{10,11... | collective-permute-start | bytes 786440 | tf_op jit(solution)/shard_map/ppermute | solution.py:140
  5.4 0.0 copy-done.2
  5.4 2.7 %collective-permute-start.2 = (bf16[32,4096]{1,0:T(8,128)(2,1)S(1)}, bf16[32,4096]{1,0:T(8,128)(2,1)S(1)}, u32[]{:S(2)}, u32[]{:S(2)}) collective-permute-start(bf16[32,4096]{1,0:T(8,128)(2,1)S(1)} %constant_dynamic-slice_fusion), channel_id=1, source_target_pairs={{0,4},{4,0},{8,12},{12,8},{1,5},{5,1},{9,13},{13,9},{2,6},{6,2},{1... | collective-permute-start | bytes 786440 | tf_op jit(solution)/shard_map/ppermute | solution.py:136
  8.1 0.0 collective-permute-done
  8.2 4.9 %all-gather = bf16[2,128,256]{2,1,0:T(8,128)(2,1)S(1)} all-gather(bf16[1,128,256]{2,1,0:T(8,128)(2,1)S(1)} %slice.18), channel_id=2, replica_groups={{0,2},{1,3},{4,6},{5,7},{8,10},{9,11},{12,14},{13,15},{16,18},{17,19},{..., dimensions={0}, use_global_device_ids=true | all-gather | bytes 196608 | tf_op jit(solution)/shard_map/all_gather | solution.py:144
  13.1 0.2 shard_map.58
  13.3 0.1 reshape.14
  13.4 2.7 %collective-permute-start.1 = (f32[2,4096]{1,0:T(2,128)S(1)}, f32[2,4096]{1,0:T(2,128)S(1)}, u32[]{:S(2)}, u32[]{:S(2)}) collective-permute-start(f32[2,4096]{1,0:T(2,128)S(1)} %reshape.14), channel_id=1, source_target_pairs={{0,8},{4,12},{8,0},{12,4},{1,9},{5,13},{9,1},{13,5},{2,10},{6,14},... | collective-permute-start | bytes 98312 | tf_op jit(solution)/shard_map/ppermute | solution.py:146
  16.1 0.0 collective-permute-done.2.mine
  16.1 0.0 collective-permute-start.3
  16.1 2.2 %collective-permute-done.1 = f32[2,4096]{1,0:T(2,128)S(1)} collective-permute-done((f32[2,4096]{1,0:T(2,128)S(1)}, f32[2,4096]{1,0:T(2,128)S(1)}, u32[]{:S(2)}, u32[]{:S(2)}) %collective-permute-start.1) | collective-permute-done | bytes 32800 | tf_op jit(solution)/shard_map/ppermute | solution.py:146
  18.4 0.0 collective-permute-done.3.other
  18.4 0.5 %shard_map.59 = f32[2,2,128]{2,1,0:T(2,128)S(1)} custom-call(f32[4,4096]{1,0:T(4,128)S(1)} %pad_maximum_fusion.1.rows, bf16[64,4096]{1,0:T(8,128)(2,1)S(1)} %copy-done.2, bf16[32,4096]{1,0:T(8,128)(2,1)S(1)} %collective-permute-done.2.mine, bf16[32,4096]{1,0:T(8,128)(2,1)S(1)} %collective-permute-done.3.other), custom_call_target="tpu_custom_call" | custom-call | flops 8388608 | bytes 524288 | tf_op jit(solution)/shard_map/pallas_call | solution.py:99
  18.8 2.8 %collective-permute-start.4 = (f32[2,128]{1,0:T(2,128)S(1)}, f32[2,128]{1,0:T(2,128)S(1)}, u32[]{:S(2)}, u32[]{:S(2)}) collective-permute-start(f32[2,128]{1,0:T(2,128)S(1)} %get-tuple-element.14), channel_id=1, source_target_pairs={{0,8},{4,12},{8,0},{12,4},{1,9},{5,13},{9,1},{13,5},{2,10},{6,14},... | collective-permute-start | bytes 3080 | tf_op jit(solution)/shard_map/ppermute | solution.py:150
  21.6 1.8 %collective-permute-done.4 = f32[2,128]{1,0:T(2,128)S(1)} collective-permute-done((f32[2,128]{1,0:T(2,128)S(1)}, f32[2,128]{1,0:T(2,128)S(1)}, u32[]{:S(2)}, u32[]{:S(2)}) %collective-permute-start.4) | collective-permute-done | bytes 1056 | tf_op jit(solution)/shard_map/ppermute | solution.py:150
  23.4 0.6 %fusion = f32[2,256]{1,0:T(2,128)} fusion(f32[2,2,128]{2,1,0:T(2,128)S(1)} %pad_maximum_fusion.2, pred[]{:T(512)S(6)} %eq.5), kind=kLoop, calls=%fused_computation.5 | loop fusion | flops 512 | bytes 4097 | tf_op jit(solution)/shard_map/reshape | solution.py:154
  (8 shorter events, 0.1 us)
Async XLA Ops:
  0.0 2.2 %copy-start = (bf16[8,128,2048]{2,1,0:T(8,128)(2,1)S(1)}, bf16[8,128,2048]{2,1,0:T(8,128)(2,1)}, u32[]{:S(2)}) copy-start(bf16[8,128,2048]{2,1,0:T(8,128)(2,1)} %param.6) | copy-start | bytes 12582916
  0.0 2.2 %copy-start.3 = (bf16[64,2048]{1,0:T(8,128)(2,1)S(1)}, bf16[64,2048]{1,0:T(8,128)(2,1)}, u32[]{:S(2)}) copy-start(bf16[64,2048]{1,0:T(8,128)(2,1)} %basis.3) | copy-start | bytes 786436
  0.0 3.5 %copy-start.1 = (bf16[8,128,2048]{2,1,0:T(8,128)(2,1)S(1)}, bf16[8,128,2048]{2,1,0:T(8,128)(2,1)}, u32[]{:S(2)}) copy-start(bf16[8,128,2048]{2,1,0:T(8,128)(2,1)} %param.5) | copy-start | bytes 12582916
  0.0 3.5 %copy-start.4 = (bf16[64,2048]{1,0:T(8,128)(2,1)S(1)}, bf16[64,2048]{1,0:T(8,128)(2,1)}, u32[]{:S(2)}) copy-start(bf16[64,2048]{1,0:T(8,128)(2,1)} %basis.2) | copy-start | bytes 786436
  2.2 3.2 %copy-start.2 = (bf16[64,4096]{1,0:T(8,128)(2,1)S(1)}, bf16[64,4096]{1,0:T(8,128)(2,1)}, u32[]{:S(2)}) copy-start(bf16[64,4096]{1,0:T(8,128)(2,1)} %near.1) | copy-start | bytes 1572868
  4.9 3.2 %collective-permute-start = (f32[2,128,256]{2,1,0:T(8,128)S(1)}, f32[2,128,256]{2,1,0:T(8,128)S(1)}, u32[]{:S(2)}, u32[]{:S(2)}) collective-permute-start(f32[2,128,256]{2,1,0:T(8,128)S(1)} %pad_maximum_fusion), channel_id=1, source_target_pairs={{0,1},{1,0},{2,3},{3,2},{4,5},{5,4},{6,7},{7,6},{8,9},{9,8},{10,11... | collective-permute-start | bytes 786440 | tf_op jit(solution)/shard_map/ppermute | solution.py:140
  5.4 10.7 %collective-permute-start.2 = (bf16[32,4096]{1,0:T(8,128)(2,1)S(1)}, bf16[32,4096]{1,0:T(8,128)(2,1)S(1)}, u32[]{:S(2)}, u32[]{:S(2)}) collective-permute-start(bf16[32,4096]{1,0:T(8,128)(2,1)S(1)} %constant_dynamic-slice_fusion), channel_id=1, source_target_pairs={{0,4},{4,0},{8,12},{12,8},{1,5},{5,1},{9,13},{13,9},{2,6},{6,2},{1... | collective-permute-start | bytes 786440 | tf_op jit(solution)/shard_map/ppermute | solution.py:136
  13.4 4.9 %collective-permute-start.1 = (f32[2,4096]{1,0:T(2,128)S(1)}, f32[2,4096]{1,0:T(2,128)S(1)}, u32[]{:S(2)}, u32[]{:S(2)}) collective-permute-start(f32[2,4096]{1,0:T(2,128)S(1)} %reshape.14), channel_id=1, source_target_pairs={{0,8},{4,12},{8,0},{12,4},{1,9},{5,13},{9,1},{13,5},{2,10},{6,14},... | collective-permute-start | bytes 98312 | tf_op jit(solution)/shard_map/ppermute | solution.py:146
  16.1 2.3 %collective-permute-start.3 = (bf16[32,4096]{1,0:T(8,128)(2,1)S(1)}, bf16[32,4096]{1,0:T(8,128)(2,1)S(1)}, u32[]{:S(2)}, u32[]{:S(2)}) collective-permute-start(bf16[32,4096]{1,0:T(8,128)(2,1)S(1)} %collective-permute-done.2.mine), channel_id=1, source_target_pairs={{0,1},{1,0},{2,3},{3,2},{4,5},{5,4},{6,7},{7,6},{8,9},{9,8},{10,11... | collective-permute-start | bytes 786440 | tf_op jit(solution)/shard_map/ppermute | solution.py:147
  18.8 4.5 %collective-permute-start.4 = (f32[2,128]{1,0:T(2,128)S(1)}, f32[2,128]{1,0:T(2,128)S(1)}, u32[]{:S(2)}, u32[]{:S(2)}) collective-permute-start(f32[2,128]{1,0:T(2,128)S(1)} %get-tuple-element.14), channel_id=1, source_target_pairs={{0,8},{4,12},{8,0},{12,4},{1,9},{5,13},{9,1},{13,5},{2,10},{6,14},... | collective-permute-start | bytes 3080 | tf_op jit(solution)/shard_map/ppermute | solution.py:150

commit v5 on v4

--- a/solution.py
+++ b/solution.py
@@ -52,10 +52,9 @@
 
 
 def outer_kernel(nx, own, scale, keep, everyone, sketch):
-    x = lax.axis_index("tensor") // 2
     mine = keep[0]
     for k in range(1, nx):
-        mine = mine + everyone[lax.rem(x + nx - k, nx), k - 1].astype(F32)
+        mine = mine + everyone[k - 1].astype(F32)
     rank, length = mine.shape[0] // 2, mine.shape[1] // own
     for s in range(own):
         part = mine[:, s * length : (s + 1) * length]
@@ -130,25 +129,30 @@
 
     near = [(at(a, b), at(a, 1 - b)) for a in range(no) for b in range(2)]
 
-    half, depth = nq // 2, queries.shape[1]
+    half = nq // 2
     part = lax.dynamic_slice_in_dim(queries, c * half, half, 0)
     token = opening()
     far_mine = lax.ppermute(part, "dp", near)
+    x = t // 2
+    pairs = [[a * 2, a * 2 + 1] for a in range(nx)]
+    columns = [[a * 2 + b for a in range(nx)] for b in range(2)]
+    outers = [[at(a, b) for a in range(no)] for b in range(2)]
+
+    def swap(value):
+        return lax.dynamic_index_in_dim(lax.all_gather(value, "tensor", axis=0, axis_index_groups=pairs), 1 - c, 0, False)
 
     give_r, keep_r = project(grads.reshape(-1, hidden), basis_out, token, nt)
     give_l, keep_l = project(acts.reshape(-1, hidden), basis_in, token, nt)
     got = lax.ppermute(jnp.concatenate([give_l, give_r], 1), "tensor", core)
     keep = jnp.concatenate([keep_l, keep_r], 1) + got
-    columns = [[a * 2 + b for a in range(nx)] for b in range(2)]
-    sent = jnp.stack([keep[k] for k in range(1, nx)], 0).astype(BF)
-    everyone = lax.all_gather(sent, "tensor", axis=0, axis_index_groups=columns)
+    arrived = [lax.ppermute(keep[k].astype(BF), "tensor", xshift(k)) for k in range(1, nx)]
+    everyone = jnp.stack(arrived, 0)
     rows = outer(keep, everyone, own).reshape(own, rank * rank)
     stacked = jnp.concatenate([rows] + [lax.ppermute(rows, "dp", oshift(k)) for k in range(1, no)], 0)
     far_other = lax.ppermute(far_mine, "tensor", core)
 
     def back(s):
         return [s[0]] + [lax.ppermute(s[k], "dp", oshift(no - k)) for k in range(1, no)]
-
     allb = jnp.stack(back(score(stacked, queries, far_mine, far_other, no, own, True)), 0)
     allb = jnp.roll(allb, o, axis=0) if no > 2 else jnp.where(o == 0, allb, allb[::-1])
     return jnp.swapaxes(allb, 0, 1).reshape(own, nd * nq)

time: 24.1 us -> 23.6 us (0.979)
  blocking collectives: 4.94 us -> 0 us
  waiting for transfers between devices: 4 us -> 6.92 us
  starting transfers between devices: 8.62 us -> 10.1 us
    all_gather x1 -> x0, blocking collectives: 4.94 us -> none  [local(): everyone = lax.all_gather(sent, 'tensor', axis=0, axis_index_groups=columns)]
    ppermute x0 -> x1, waiting for transfers between devices: none -> 2.77 us  [local(): lax.ppermute(keep[k].astype(BF), 'tensor', xshift(k))]
    ppermute x0 -> x1, starting transfers between devices: none -> 1.56 us  [local(): lax.ppermute(keep[k].astype(BF), 'tensor', xshift(k))]
  transfers between devices with their start and end apart: 5 -> 6, of which waited for: 2 -> 3; matrix products, arithmetic and copies ran while one was open for 1% -> 1% of each run, Pallas kernels for 1% -> 1%
where the time goes in v5:
time: 23.6 us; the launch traced here: 23.4 us
  starting transfers between devices  10.1 us (43%)
  waiting for transfers between devices  6.92 us (29%)
  Pallas kernels  3.26 us (14%)
  local copies, waits for them, and re-layouts  2.39 us (10%)
  other arithmetic  0.68 us (3%)
    ppermute x1, waiting for transfers between devices, local(): lax.ppermute(keep[k].astype(BF), 'tensor', xshift(k))  2.77 us
    ppermute x1, starting transfers between devices, back(): lax.ppermute(s[k], 'dp', oshift(no - k))  2.69 us
    ppermute x1, starting transfers between devices, local(): far_mine = lax.ppermute(part, 'dp', near)  2.68 us
    ppermute x1, starting transfers between devices, local(): lax.ppermute(rows, 'dp', oshift(k))  2.65 us
    pallas_call x2, Pallas kernels, project(): pl.pallas_call(functools.partial(project_kernel, nx, nt), out_shape=[shap...  2.6 us
    ppermute x1, waiting for transfers between devices, local(): lax.ppermute(rows, 'dp', oshift(k))  2.29 us
    unnamed x10, local copies, waits for them, and re-layouts  2.24 us
    ppermute x1, waiting for transfers between devices, back(): lax.ppermute(s[k], 'dp', oshift(no - k))  1.85 us
  transfers between devices with their start and end apart: 6, of which 3 were waited for; matrix products, arithmetic and copies ran while one was open for 1% of the time, Pallas kernels for 1%

profile of v5, /device:TPU:0, one launch (start us, length us, event | category | flops | bytes accessed | tf_op | source)
XLA Modules:
  0.0 23.4 jit_solution(2537734203138117830)
XLA Ops:
  0.0 0.0 copy-start
  0.0 0.0 copy-start.3
  0.0 0.0 copy-start.1
  0.0 0.0 copy-start.4
  0.0 2.2 %copy-done = bf16[8,128,2048]{2,1,0:T(8,128)(2,1)S(1)} copy-done((bf16[8,128,2048]{2,1,0:T(8,128)(2,1)S(1)}, bf16[8,128,2048]{2,1,0:T(8,128)(2,1)}, u32[]{:S(2)}) %copy-start) | copy-done | bytes 4194328
  2.2 0.0 copy-done.3
  2.2 0.0 copy-start.2
  2.2 1.3 %shard_map.57 = (f32[2,64,256]{2,1,0:T(8,128)S(1)}, f32[2,64,256]{2,1,0:T(8,128)S(1)}) custom-call(bf16[1024,2048]{1,0:T(8,128)(2,1)S(1)} %bitcast.12, bf16[64,2048]{1,0:T(8,128)(2,1)S(1)} %copy-done.3, f32[8,128]{1,0:T(8,128)S(1)} %shard_map.55.token), custom_call_target="tpu_custom_call" | custom-call | flops 268435456 | bytes 4194304 | tf_op jit(solution)/shard_map/pallas_call | solution.py:44
  3.5 0.0 copy-done.1
  3.5 0.0 copy-done.4
  3.5 1.3 %shard_map.56 = (f32[2,64,256]{2,1,0:T(8,128)S(1)}, f32[2,64,256]{2,1,0:T(8,128)S(1)}) custom-call(bf16[1024,2048]{1,0:T(8,128)(2,1)S(1)} %bitcast.13, bf16[64,2048]{1,0:T(8,128)(2,1)S(1)} %copy-done.4, f32[8,128]{1,0:T(8,128)S(1)} %shard_map.55.token), custom_call_target="tpu_custom_call" | custom-call | flops 268435456 | bytes 4194304 | tf_op jit(solution)/shard_map/pallas_call | solution.py:44
  4.9 0.5 %collective-permute-start = (f32[2,128,256]{2,1,0:T(8,128)S(1)}, f32[2,128,256]{2,1,0:T(8,128)S(1)}, u32[]{:S(2)}, u32[]{:S(2)}) collective-permute-start(f32[2,128,256]{2,1,0:T(8,128)S(1)} %pad_maximum_fusion), channel_id=1, source_target_pairs={{0,1},{1,0},{2,3},{3,2},{4,5},{5,4},{6,7},{7,6},{8,9},{9,8},{10,11... | collective-permute-start | bytes 786440 | tf_op jit(solution)/shard_map/ppermute | solution.py:146
  5.4 0.0 copy-done.2
  5.4 2.7 %collective-permute-start.3 = (bf16[32,4096]{1,0:T(8,128)(2,1)S(1)}, bf16[32,4096]{1,0:T(8,128)(2,1)S(1)}, u32[]{:S(2)}, u32[]{:S(2)}) collective-permute-start(bf16[32,4096]{1,0:T(8,128)(2,1)S(1)} %constant_dynamic-slice_fusion), channel_id=1, source_target_pairs={{0,4},{4,0},{8,12},{12,8},{1,5},{5,1},{9,13},{13,9},{2,6},{6,2},{1... | collective-permute-start | bytes 786440 | tf_op jit(solution)/shard_map/ppermute | solution.py:135
  8.1 0.0 collective-permute-done
  8.2 1.6 %collective-permute-start.1 = (bf16[128,256]{1,0:T(8,128)(2,1)S(1)}, bf16[128,256]{1,0:T(8,128)(2,1)S(1)}, u32[]{:S(2)}, u32[]{:S(2)}) collective-permute-start(bf16[128,256]{1,0:T(8,128)(2,1)S(1)} %fusion), channel_id=1, source_target_pairs={{0,2},{1,3},{2,0},{3,1},{4,6},{5,7},{6,4},{7,5},{8,10},{9,11},{10,... | collective-permute-start | bytes 196616 | tf_op jit(solution)/shard_map/ppermute | solution.py:148
  9.7 2.8 %collective-permute-done.1 = bf16[128,256]{1,0:T(8,128)(2,1)S(1)} collective-permute-done((bf16[128,256]{1,0:T(8,128)(2,1)S(1)}, bf16[128,256]{1,0:T(8,128)(2,1)S(1)}, u32[]{:S(2)}, u32[]{:S(2)}) %collective-permute-start.1) | collective-permute-done | bytes 65568 | tf_op jit(solution)/shard_map/ppermute | solution.py:148
  12.5 0.2 shard_map.58
  12.7 0.1 reshape.15
  12.8 2.7 %collective-permute-start.2 = (f32[2,4096]{1,0:T(2,128)S(1)}, f32[2,4096]{1,0:T(2,128)S(1)}, u32[]{:S(2)}, u32[]{:S(2)}) collective-permute-start(f32[2,4096]{1,0:T(2,128)S(1)} %reshape.15), channel_id=1, source_target_pairs={{0,8},{4,12},{8,0},{12,4},{1,9},{5,13},{9,1},{13,5},{2,10},{6,14},... | collective-permute-start | bytes 98312 | tf_op jit(solution)/shard_map/ppermute | solution.py:151
  15.5 0.0 collective-permute-done.3.mine
  15.5 0.0 collective-permute-start.4
  15.5 2.3 %collective-permute-done.2 = f32[2,4096]{1,0:T(2,128)S(1)} collective-permute-done((f32[2,4096]{1,0:T(2,128)S(1)}, f32[2,4096]{1,0:T(2,128)S(1)}, u32[]{:S(2)}, u32[]{:S(2)}) %collective-permute-start.2) | collective-permute-done | bytes 32800 | tf_op jit(solution)/shard_map/ppermute | solution.py:151
  17.8 0.0 collective-permute-done.4.other
  17.8 0.5 %shard_map.59 = f32[2,2,128]{2,1,0:T(2,128)S(1)} custom-call(f32[4,4096]{1,0:T(4,128)S(1)} %pad_maximum_fusion.1.rows, bf16[64,4096]{1,0:T(8,128)(2,1)S(1)} %copy-done.2, bf16[32,4096]{1,0:T(8,128)(2,1)S(1)} %collective-permute-done.3.mine, bf16[32,4096]{1,0:T(8,128)(2,1)S(1)} %collective-permute-done.4.other), custom_call_target="tpu_custom_call" | custom-call | flops 8388608 | bytes 524288 | tf_op jit(solution)/shard_map/pallas_call | solution.py:98
  18.3 2.7 %collective-permute-start.5 = (f32[2,128]{1,0:T(2,128)S(1)}, f32[2,128]{1,0:T(2,128)S(1)}, u32[]{:S(2)}, u32[]{:S(2)}) collective-permute-start(f32[2,128]{1,0:T(2,128)S(1)} %get-tuple-element.14), channel_id=1, source_target_pairs={{0,8},{4,12},{8,0},{12,4},{1,9},{5,13},{9,1},{13,5},{2,10},{6,14},... | collective-permute-start | bytes 3080 | tf_op jit(solution)/shard_map/ppermute | solution.py:155
  21.0 1.8 %collective-permute-done.5 = f32[2,128]{1,0:T(2,128)S(1)} collective-permute-done((f32[2,128]{1,0:T(2,128)S(1)}, f32[2,128]{1,0:T(2,128)S(1)}, u32[]{:S(2)}, u32[]{:S(2)}) %collective-permute-start.5) | collective-permute-done | bytes 1056 | tf_op jit(solution)/shard_map/ppermute | solution.py:155
  22.8 0.6 %fusion.1 = f32[2,256]{1,0:T(2,128)} fusion(f32[2,2,128]{2,1,0:T(2,128)S(1)} %pad_maximum_fusion.2, pred[]{:T(512)S(6)} %eq.5), kind=kLoop, calls=%fused_computation.6 | loop fusion | flops 512 | bytes 4097 | tf_op jit(solution)/shard_map/reshape | solution.py:158
  (8 shorter events, 0.1 us)
Async XLA Ops:
  0.0 2.2 %copy-start = (bf16[8,128,2048]{2,1,0:T(8,128)(2,1)S(1)}, bf16[8,128,2048]{2,1,0:T(8,128)(2,1)}, u32[]{:S(2)}) copy-start(bf16[8,128,2048]{2,1,0:T(8,128)(2,1)} %param.6) | copy-start | bytes 12582916
  0.0 2.2 %copy-start.3 = (bf16[64,2048]{1,0:T(8,128)(2,1)S(1)}, bf16[64,2048]{1,0:T(8,128)(2,1)}, u32[]{:S(2)}) copy-start(bf16[64,2048]{1,0:T(8,128)(2,1)} %basis.3) | copy-start | bytes 786436
  0.0 3.5 %copy-start.1 = (bf16[8,128,2048]{2,1,0:T(8,128)(2,1)S(1)}, bf16[8,128,2048]{2,1,0:T(8,128)(2,1)}, u32[]{:S(2)}) copy-start(bf16[8,128,2048]{2,1,0:T(8,128)(2,1)} %param.5) | copy-start | bytes 12582916
  0.0 3.5 %copy-start.4 = (bf16[64,2048]{1,0:T(8,128)(2,1)S(1)}, bf16[64,2048]{1,0:T(8,128)(2,1)}, u32[]{:S(2)}) copy-start(bf16[64,2048]{1,0:T(8,128)(2,1)} %basis.2) | copy-start | bytes 786436
  2.2 3.2 %copy-start.2 = (bf16[64,4096]{1,0:T(8,128)(2,1)S(1)}, bf16[64,4096]{1,0:T(8,128)(2,1)}, u32[]{:S(2)}) copy-start(bf16[64,4096]{1,0:T(8,128)(2,1)} %near.1) | copy-start | bytes 1572868
  4.9 3.2 %collective-permute-start = (f32[2,128,256]{2,1,0:T(8,128)S(1)}, f32[2,128,256]{2,1,0:T(8,128)S(1)}, u32[]{:S(2)}, u32[]{:S(2)}) collective-permute-start(f32[2,128,256]{2,1,0:T(8,128)S(1)} %pad_maximum_fusion), channel_id=1, source_target_pairs={{0,1},{1,0},{2,3},{3,2},{4,5},{5,4},{6,7},{7,6},{8,9},{9,8},{10,11... | collective-permute-start | bytes 786440 | tf_op jit(solution)/shard_map/ppermute | solution.py:146
  5.4 10.1 %collective-permute-start.3 = (bf16[32,4096]{1,0:T(8,128)(2,1)S(1)}, bf16[32,4096]{1,0:T(8,128)(2,1)S(1)}, u32[]{:S(2)}, u32[]{:S(2)}) collective-permute-start(bf16[32,4096]{1,0:T(8,128)(2,1)S(1)} %constant_dynamic-slice_fusion), channel_id=1, source_target_pairs={{0,4},{4,0},{8,12},{12,8},{1,5},{5,1},{9,13},{13,9},{2,6},{6,2},{1... | collective-permute-start | bytes 786440 | tf_op jit(solution)/shard_map/ppermute | solution.py:135
  8.2 4.3 %collective-permute-start.1 = (bf16[128,256]{1,0:T(8,128)(2,1)S(1)}, bf16[128,256]{1,0:T(8,128)(2,1)S(1)}, u32[]{:S(2)}, u32[]{:S(2)}) collective-permute-start(bf16[128,256]{1,0:T(8,128)(2,1)S(1)} %fusion), channel_id=1, source_target_pairs={{0,2},{1,3},{2,0},{3,1},{4,6},{5,7},{6,4},{7,5},{8,10},{9,11},{10,... | collective-permute-start | bytes 196616 | tf_op jit(solution)/shard_map/ppermute | solution.py:148
  12.8 5.0 %collective-permute-start.2 = (f32[2,4096]{1,0:T(2,128)S(1)}, f32[2,4096]{1,0:T(2,128)S(1)}, u32[]{:S(2)}, u32[]{:S(2)}) collective-permute-start(f32[2,4096]{1,0:T(2,128)S(1)} %reshape.15), channel_id=1, source_target_pairs={{0,8},{4,12},{8,0},{12,4},{1,9},{5,13},{9,1},{13,5},{2,10},{6,14},... | collective-permute-start | bytes 98312 | tf_op jit(solution)/shard_map/ppermute | solution.py:151
  15.5 2.3 %collective-permute-start.4 = (bf16[32,4096]{1,0:T(8,128)(2,1)S(1)}, bf16[32,4096]{1,0:T(8,128)(2,1)S(1)}, u32[]{:S(2)}, u32[]{:S(2)}) collective-permute-start(bf16[32,4096]{1,0:T(8,128)(2,1)S(1)} %collective-permute-done.3.mine), channel_id=1, source_target_pairs={{0,1},{1,0},{2,3},{3,2},{4,5},{5,4},{6,7},{7,6},{8,9},{9,8},{10,11... | collective-permute-start | bytes 786440 | tf_op jit(solution)/shard_map/ppermute | solution.py:152
  18.3 4.5 %collective-permute-start.5 = (f32[2,128]{1,0:T(2,128)S(1)}, f32[2,128]{1,0:T(2,128)S(1)}, u32[]{:S(2)}, u32[]{:S(2)}) collective-permute-start(f32[2,128]{1,0:T(2,128)S(1)} %get-tuple-element.14), channel_id=1, source_target_pairs={{0,8},{4,12},{8,0},{12,4},{1,9},{5,13},{9,1},{13,5},{2,10},{6,14},... | collective-permute-start | bytes 3080 | tf_op jit(solution)/shard_map/ppermute | solution.py:155

commit v6 on v5

--- a/solution.py
+++ b/solution.py
@@ -19,13 +19,17 @@
         open_kernel,
         out_shape=jax.ShapeDtypeStruct((8, 128), F32),
         out_specs=pl.BlockSpec(memory_space=pltpu.VMEM),
-        compiler_params=pltpu.CompilerParams(vmem_limit_bytes=16 * 2**20),
+        compiler_params=pltpu.CompilerParams(vmem_limit_bytes=4 * 2**20),
         cost_estimate=pl.CostEstimate(flops=10000000000, bytes_accessed=0, transcendentals=0),
     )()
 
 
-def project_kernel(nx, nt, values, basis, token, give, keep):
-    rows = give.shape[2]
+def project_kernel(nx, nt, values, basis, token, *refs):
+    give, keep = refs[-2:]
+    rank, rows = basis.shape[0], give.shape[2]
+    if len(refs) > 2:
+        give[:, rank:] = refs[0][...]
+        keep[:, rank:] = refs[1][...]
     t = lax.axis_index("tensor")
     x, c = t // 2, t % 2
     for j in range(nt):
@@ -33,22 +37,22 @@
         place = lax.rem(x + k, nx) * 2 + ((1 - c) if other else c)
         source = pl.ds(pl.multiple_of(place * rows, rows), rows)
         to = give if other else keep
-        to[k] = lax.dot_general(values[source], basis[...], (((1,), (1,)), ((), ())), preferred_element_type=F32).T
+        to[k, :rank] = lax.dot_general(values[source], basis[...], (((1,), (1,)), ((), ())), preferred_element_type=F32).T
 
 
-def project(values, basis, token, nt):
+def project(values, basis, token, nt, *others):
     rank, hidden = basis.shape
     rows = values.shape[0] // nt
     nx = nt // 2
-    shape = jax.ShapeDtypeStruct((nx, rank, rows), F32)
+    shape = jax.ShapeDtypeStruct((nx, 2 * rank if others else rank, rows), F32)
     return pl.pallas_call(
         functools.partial(project_kernel, nx, nt),
         out_shape=[shape, shape],
-        in_specs=[pl.BlockSpec(memory_space=pltpu.VMEM)] * 3,
+        in_specs=[pl.BlockSpec(memory_space=pltpu.VMEM)] * (3 + len(others)),
         out_specs=[pl.BlockSpec(memory_space=pltpu.VMEM)] * 2,
-        compiler_params=pltpu.CompilerParams(vmem_limit_bytes=16 * 2**20),
+        compiler_params=pltpu.CompilerParams(vmem_limit_bytes=4 * 2**20),
         cost_estimate=pl.CostEstimate(flops=2 * nt * rows * hidden * rank, bytes_accessed=2 * nt * rows * hidden, transcendentals=0),
-    )(values, basis, token)
+    )(values, basis, token, *others)
 
 
 def outer_kernel(nx, own, scale, keep, everyone, sketch):
@@ -71,7 +75,7 @@
         out_shape=jax.ShapeDtypeStruct((own, rank, rank), F32),
         in_specs=[pl.BlockSpec(memory_space=pltpu.VMEM)] * 2,
         out_specs=pl.BlockSpec(memory_space=pltpu.VMEM),
-        compiler_params=pltpu.CompilerParams(vmem_limit_bytes=16 * 2**20),
+        compiler_params=pltpu.CompilerParams(vmem_limit_bytes=4 * 2**20),
         cost_estimate=pl.CostEstimate(flops=12 * rank * rank * tokens, bytes_accessed=4 * keep.size, transcendentals=0),
     )(keep, everyone)
 
@@ -100,7 +104,7 @@
         out_shape=jax.ShapeDtypeStruct((no, own, 2 * near.shape[0]), F32),
         in_specs=[pl.BlockSpec(memory_space=pltpu.VMEM)] * 4,
         out_specs=pl.BlockSpec(memory_space=pltpu.VMEM),
-        compiler_params=pltpu.CompilerParams(vmem_limit_bytes=16 * 2**20),
+        compiler_params=pltpu.CompilerParams(vmem_limit_bytes=4 * 2**20),
         cost_estimate=pl.CostEstimate(flops=8 * rows.size * near.shape[0], bytes_accessed=2 * near.size, transcendentals=0),
     )(rows, near, mine, other)
 
@@ -141,10 +145,10 @@
     def swap(value):
         return lax.dynamic_index_in_dim(lax.all_gather(value, "tensor", axis=0, axis_index_groups=pairs), 1 - c, 0, False)
 
-    give_r, keep_r = project(grads.reshape(-1, hidden), basis_out, token, nt)
-    give_l, keep_l = project(acts.reshape(-1, hidden), basis_in, token, nt)
-    got = lax.ppermute(jnp.concatenate([give_l, give_r], 1), "tensor", core)
-    keep = jnp.concatenate([keep_l, keep_r], 1) + got
+    give, keep = project(grads.reshape(-1, hidden), basis_out, token, nt)
+    give, keep = project(acts.reshape(-1, hidden), basis_in, token, nt, give, keep)
+    got = lax.ppermute(give, "tensor", core)
+    keep = keep + got
     arrived = [lax.ppermute(keep[k].astype(BF), "tensor", xshift(k)) for k in range(1, nx)]
     everyone = jnp.stack(arrived, 0)
     rows = outer(keep, everyone, own).reshape(own, rank * rank)

time: 23.6 us -> 23.5 us (level)
  no operation moved by 1% of the time
where the time goes in v6:
time: 23.5 us; the launch traced here: 23.4 us
  starting transfers between devices  10.1 us (43%)
  waiting for transfers between devices  6.92 us (29%)
  Pallas kernels  3.27 us (14%)
  local copies, waits for them, and re-layouts  2.39 us (10%)
  other arithmetic  0.65 us (3%)
    ppermute x1, waiting for transfers between devices, local(): lax.ppermute(keep[k].astype(BF), 'tensor', xshift(k))  2.77 us
    ppermute x1, starting transfers between devices, back(): lax.ppermute(s[k], 'dp', oshift(no - k))  2.69 us
    ppermute x1, starting transfers between devices, local(): far_mine = lax.ppermute(part, 'dp', near)  2.68 us
    ppermute x1, starting transfers between devices, local(): lax.ppermute(rows, 'dp', oshift(k))  2.65 us
    pallas_call x2, Pallas kernels, project(): pl.pallas_call(functools.partial(project_kernel, nx, nt), out_shape=[shap...  2.6 us
    ppermute x1, waiting for transfers between devices, local(): lax.ppermute(rows, 'dp', oshift(k))  2.29 us
    unnamed x10, local copies, waits for them, and re-layouts  2.24 us
    ppermute x1, waiting for transfers between devices, back(): lax.ppermute(s[k], 'dp', oshift(no - k))  1.85 us
  transfers between devices with their start and end apart: 6, of which 3 were waited for; matrix products, arithmetic and copies ran while one was open for 1% of the time, Pallas kernels for 1%

profile of v6, /device:TPU:0, one launch (start us, length us, event | category | flops | bytes accessed | tf_op | source)
XLA Modules:
  0.0 23.4 jit_solution(13777299142634114497)
XLA Ops:
  0.0 0.0 copy-start
  0.0 0.0 copy-start.3
  0.0 0.0 copy-start.1
  0.0 0.0 copy-start.4
  0.0 2.2 %copy-done = bf16[8,128,2048]{2,1,0:T(8,128)(2,1)S(1)} copy-done((bf16[8,128,2048]{2,1,0:T(8,128)(2,1)S(1)}, bf16[8,128,2048]{2,1,0:T(8,128)(2,1)}, u32[]{:S(2)}) %copy-start) | copy-done | bytes 4194328
  2.2 0.0 copy-done.3
  2.2 0.0 copy-start.2
  2.2 1.3 %shard_map.56 = (f32[2,64,256]{2,1,0:T(8,128)S(1)}, f32[2,64,256]{2,1,0:T(8,128)S(1)}) custom-call(bf16[1024,2048]{1,0:T(8,128)(2,1)S(1)} %bitcast.12, bf16[64,2048]{1,0:T(8,128)(2,1)S(1)} %copy-done.3, f32[8,128]{1,0:T(8,128)S(1)} %shard_map.55.token), custom_call_target="tpu_custom_call" | custom-call | flops 268435456 | bytes 4194304 | tf_op jit(solution)/shard_map/pallas_call | solution.py:48
  3.5 0.0 copy-done.1
  3.5 0.0 copy-done.4
  3.5 1.3 %shard_map.57 = (f32[2,128,256]{2,1,0:T(8,128)S(1)}, f32[2,128,256]{2,1,0:T(8,128)S(1)}) custom-call(bf16[1024,2048]{1,0:T(8,128)(2,1)S(1)} %bitcast.13, bf16[64,2048]{1,0:T(8,128)(2,1)S(1)} %copy-done.4, f32[8,128]{1,0:T(8,128)S(1)} %shard_map.55.token, f32[2,64,256]{2,1,0:T(8,128)S(1)} %get-tuple-element.9.refs_0_, f32[2,64,256]{2,1,0:T(8,128)S(1)} %get-tuple-element.10.refs_1_), custom_call_target="tpu_custom_call" | custom-call | flops 268435456 | bytes 4194304 | tf_op jit(solution)/shard_map/pallas_call | solution.py:48
  4.8 0.5 %collective-permute-start = (f32[2,128,256]{2,1,0:T(8,128)S(1)}, f32[2,128,256]{2,1,0:T(8,128)S(1)}, u32[]{:S(2)}, u32[]{:S(2)}) collective-permute-start(f32[2,128,256]{2,1,0:T(8,128)S(1)} %get-tuple-element.12), channel_id=1, source_target_pairs={{0,1},{1,0},{2,3},{3,2},{4,5},{5,4},{6,7},{7,6},{8,9},{9,8},{10,11... | collective-permute-start | bytes 786440 | tf_op jit(solution)/shard_map/ppermute | solution.py:150
  5.4 0.0 copy-done.2
  5.4 2.7 %collective-permute-start.3 = (bf16[32,4096]{1,0:T(8,128)(2,1)S(1)}, bf16[32,4096]{1,0:T(8,128)(2,1)S(1)}, u32[]{:S(2)}, u32[]{:S(2)}) collective-permute-start(bf16[32,4096]{1,0:T(8,128)(2,1)S(1)} %constant_dynamic-slice_fusion), channel_id=1, source_target_pairs={{0,4},{4,0},{8,12},{12,8},{1,5},{5,1},{9,13},{13,9},{2,6},{6,2},{1... | collective-permute-start | bytes 786440 | tf_op jit(solution)/shard_map/ppermute | solution.py:139
  8.1 0.0 collective-permute-done
  8.1 1.6 %collective-permute-start.1 = (bf16[128,256]{1,0:T(8,128)(2,1)S(1)}, bf16[128,256]{1,0:T(8,128)(2,1)S(1)}, u32[]{:S(2)}, u32[]{:S(2)}) collective-permute-start(bf16[128,256]{1,0:T(8,128)(2,1)S(1)} %fusion), channel_id=1, source_target_pairs={{0,2},{1,3},{2,0},{3,1},{4,6},{5,7},{6,4},{7,5},{8,10},{9,11},{10,... | collective-permute-start | bytes 196616 | tf_op jit(solution)/shard_map/ppermute | solution.py:152
  9.7 2.8 %collective-permute-done.1 = bf16[128,256]{1,0:T(8,128)(2,1)S(1)} collective-permute-done((bf16[128,256]{1,0:T(8,128)(2,1)S(1)}, bf16[128,256]{1,0:T(8,128)(2,1)S(1)}, u32[]{:S(2)}, u32[]{:S(2)}) %collective-permute-start.1) | collective-permute-done | bytes 65568 | tf_op jit(solution)/shard_map/ppermute | solution.py:152
  12.5 0.2 shard_map.58
  12.7 0.1 reshape.15
  12.8 2.7 %collective-permute-start.2 = (f32[2,4096]{1,0:T(2,128)S(1)}, f32[2,4096]{1,0:T(2,128)S(1)}, u32[]{:S(2)}, u32[]{:S(2)}) collective-permute-start(f32[2,4096]{1,0:T(2,128)S(1)} %reshape.15), channel_id=1, source_target_pairs={{0,8},{4,12},{8,0},{12,4},{1,9},{5,13},{9,1},{13,5},{2,10},{6,14},... | collective-permute-start | bytes 98312 | tf_op jit(solution)/shard_map/ppermute | solution.py:155
  15.5 0.0 collective-permute-done.3.mine
  15.5 0.0 collective-permute-start.4
  15.5 2.3 %collective-permute-done.2 = f32[2,4096]{1,0:T(2,128)S(1)} collective-permute-done((f32[2,4096]{1,0:T(2,128)S(1)}, f32[2,4096]{1,0:T(2,128)S(1)}, u32[]{:S(2)}, u32[]{:S(2)}) %collective-permute-start.2) | collective-permute-done | bytes 32800 | tf_op jit(solution)/shard_map/ppermute | solution.py:155
  17.8 0.0 collective-permute-done.4.other
  17.8 0.5 %shard_map.59 = f32[2,2,128]{2,1,0:T(2,128)S(1)} custom-call(f32[4,4096]{1,0:T(4,128)S(1)} %pad_maximum_fusion.rows, bf16[64,4096]{1,0:T(8,128)(2,1)S(1)} %copy-done.2, bf16[32,4096]{1,0:T(8,128)(2,1)S(1)} %collective-permute-done.3.mine, bf16[32,4096]{1,0:T(8,128)(2,1)S(1)} %collective-permute-done.4.other), custom_call_target="tpu_custom_call" | custom-call | flops 8388608 | bytes 524288 | tf_op jit(solution)/shard_map/pallas_call | solution.py:102
  18.3 2.7 %collective-permute-start.5 = (f32[2,128]{1,0:T(2,128)S(1)}, f32[2,128]{1,0:T(2,128)S(1)}, u32[]{:S(2)}, u32[]{:S(2)}) collective-permute-start(f32[2,128]{1,0:T(2,128)S(1)} %get-tuple-element.14), channel_id=1, source_target_pairs={{0,8},{4,12},{8,0},{12,4},{1,9},{5,13},{9,1},{13,5},{2,10},{6,14},... | collective-permute-start | bytes 3080 | tf_op jit(solution)/shard_map/ppermute | solution.py:159
  21.0 1.8 %collective-permute-done.5 = f32[2,128]{1,0:T(2,128)S(1)} collective-permute-done((f32[2,128]{1,0:T(2,128)S(1)}, f32[2,128]{1,0:T(2,128)S(1)}, u32[]{:S(2)}, u32[]{:S(2)}) %collective-permute-start.5) | collective-permute-done | bytes 1056 | tf_op jit(solution)/shard_map/ppermute | solution.py:159
  22.8 0.6 %fusion.1 = f32[2,256]{1,0:T(2,128)} fusion(f32[2,2,128]{2,1,0:T(2,128)S(1)} %pad_maximum_fusion.1, pred[]{:T(512)S(6)} %eq.5), kind=kLoop, calls=%fused_computation.4 | loop fusion | flops 512 | bytes 4097 | tf_op jit(solution)/shard_map/reshape | solution.py:162
  (7 shorter events, 0.1 us)
Async XLA Ops:
  0.0 2.2 %copy-start = (bf16[8,128,2048]{2,1,0:T(8,128)(2,1)S(1)}, bf16[8,128,2048]{2,1,0:T(8,128)(2,1)}, u32[]{:S(2)}) copy-start(bf16[8,128,2048]{2,1,0:T(8,128)(2,1)} %param.6) | copy-start | bytes 12582916
  0.0 2.2 %copy-start.3 = (bf16[64,2048]{1,0:T(8,128)(2,1)S(1)}, bf16[64,2048]{1,0:T(8,128)(2,1)}, u32[]{:S(2)}) copy-start(bf16[64,2048]{1,0:T(8,128)(2,1)} %basis.2) | copy-start | bytes 786436
  0.0 3.5 %copy-start.1 = (bf16[8,128,2048]{2,1,0:T(8,128)(2,1)S(1)}, bf16[8,128,2048]{2,1,0:T(8,128)(2,1)}, u32[]{:S(2)}) copy-start(bf16[8,128,2048]{2,1,0:T(8,128)(2,1)} %param.5) | copy-start | bytes 12582916
  0.0 3.5 %copy-start.4 = (bf16[64,2048]{1,0:T(8,128)(2,1)S(1)}, bf16[64,2048]{1,0:T(8,128)(2,1)}, u32[]{:S(2)}) copy-start(bf16[64,2048]{1,0:T(8,128)(2,1)} %basis.3) | copy-start | bytes 786436
  2.2 3.2 %copy-start.2 = (bf16[64,4096]{1,0:T(8,128)(2,1)S(1)}, bf16[64,4096]{1,0:T(8,128)(2,1)}, u32[]{:S(2)}) copy-start(bf16[64,4096]{1,0:T(8,128)(2,1)} %near.1) | copy-start | bytes 1572868
  4.8 3.2 %collective-permute-start = (f32[2,128,256]{2,1,0:T(8,128)S(1)}, f32[2,128,256]{2,1,0:T(8,128)S(1)}, u32[]{:S(2)}, u32[]{:S(2)}) collective-permute-start(f32[2,128,256]{2,1,0:T(8,128)S(1)} %get-tuple-element.12), channel_id=1, source_target_pairs={{0,1},{1,0},{2,3},{3,2},{4,5},{5,4},{6,7},{7,6},{8,9},{9,8},{10,11... | collective-permute-start | bytes 786440 | tf_op jit(solution)/shard_map/ppermute | solution.py:150
  5.4 10.1 %collective-permute-start.3 = (bf16[32,4096]{1,0:T(8,128)(2,1)S(1)}, bf16[32,4096]{1,0:T(8,128)(2,1)S(1)}, u32[]{:S(2)}, u32[]{:S(2)}) collective-permute-start(bf16[32,4096]{1,0:T(8,128)(2,1)S(1)} %constant_dynamic-slice_fusion), channel_id=1, source_target_pairs={{0,4},{4,0},{8,12},{12,8},{1,5},{5,1},{9,13},{13,9},{2,6},{6,2},{1... | collective-permute-start | bytes 786440 | tf_op jit(solution)/shard_map/ppermute | solution.py:139
  8.1 4.3 %collective-permute-start.1 = (bf16[128,256]{1,0:T(8,128)(2,1)S(1)}, bf16[128,256]{1,0:T(8,128)(2,1)S(1)}, u32[]{:S(2)}, u32[]{:S(2)}) collective-permute-start(bf16[128,256]{1,0:T(8,128)(2,1)S(1)} %fusion), channel_id=1, source_target_pairs={{0,2},{1,3},{2,0},{3,1},{4,6},{5,7},{6,4},{7,5},{8,10},{9,11},{10,... | collective-permute-start | bytes 196616 | tf_op jit(solution)/shard_map/ppermute | solution.py:152
  12.8 4.9 %collective-permute-start.2 = (f32[2,4096]{1,0:T(2,128)S(1)}, f32[2,4096]{1,0:T(2,128)S(1)}, u32[]{:S(2)}, u32[]{:S(2)}) collective-permute-start(f32[2,4096]{1,0:T(2,128)S(1)} %reshape.15), channel_id=1, source_target_pairs={{0,8},{4,12},{8,0},{12,4},{1,9},{5,13},{9,1},{13,5},{2,10},{6,14},... | collective-permute-start | bytes 98312 | tf_op jit(solution)/shard_map/ppermute | solution.py:155
  15.5 2.3 %collective-permute-start.4 = (bf16[32,4096]{1,0:T(8,128)(2,1)S(1)}, bf16[32,4096]{1,0:T(8,128)(2,1)S(1)}, u32[]{:S(2)}, u32[]{:S(2)}) collective-permute-start(bf16[32,4096]{1,0:T(8,128)(2,1)S(1)} %collective-permute-done.3.mine), channel_id=1, source_target_pairs={{0,1},{1,0},{2,3},{3,2},{4,5},{5,4},{6,7},{7,6},{8,9},{9,8},{10,11... | collective-permute-start | bytes 786440 | tf_op jit(solution)/shard_map/ppermute | solution.py:156
  18.3 4.5 %collective-permute-start.5 = (f32[2,128]{1,0:T(2,128)S(1)}, f32[2,128]{1,0:T(2,128)S(1)}, u32[]{:S(2)}, u32[]{:S(2)}) collective-permute-start(f32[2,128]{1,0:T(2,128)S(1)} %get-tuple-element.14), channel_id=1, source_target_pairs={{0,8},{4,12},{8,0},{12,4},{1,9},{5,13},{9,1},{13,5},{2,10},{6,14},... | collective-permute-start | bytes 3080 | tf_op jit(solution)/shard_map/ppermute | solution.py:159

commit v7 on v6

--- a/solution.py
+++ b/solution.py
@@ -55,8 +55,8 @@
     )(values, basis, token, *others)
 
 
-def outer_kernel(nx, own, scale, keep, everyone, sketch):
-    mine = keep[0]
+def outer_kernel(nx, own, scale, keep, got, everyone, sketch):
+    mine = keep[0] + got[0]
     for k in range(1, nx):
         mine = mine + everyone[k - 1].astype(F32)
     rank, length = mine.shape[0] // 2, mine.shape[1] // own
@@ -67,17 +67,17 @@
         )
 
 
-def outer(keep, everyone, own):
+def outer(keep, got, everyone, own):
     nx, twice, tokens = keep.shape
     rank = twice // 2
     return pl.pallas_call(
         functools.partial(outer_kernel, nx, own, 1.0 / (tokens // own * rank)),
         out_shape=jax.ShapeDtypeStruct((own, rank, rank), F32),
-        in_specs=[pl.BlockSpec(memory_space=pltpu.VMEM)] * 2,
+        in_specs=[pl.BlockSpec(memory_space=pltpu.VMEM)] * 3,
         out_specs=pl.BlockSpec(memory_space=pltpu.VMEM),
         compiler_params=pltpu.CompilerParams(vmem_limit_bytes=4 * 2**20),
         cost_estimate=pl.CostEstimate(flops=12 * rank * rank * tokens, bytes_accessed=4 * keep.size, transcendentals=0),
-    )(keep, everyone)
+    )(keep, got, everyone)
 
 
 def score_kernel(no, own, outer_axis, rows, near, mine, other, out):
@@ -148,10 +148,9 @@
     give, keep = project(grads.reshape(-1, hidden), basis_out, token, nt)
     give, keep = project(acts.reshape(-1, hidden), basis_in, token, nt, give, keep)
     got = lax.ppermute(give, "tensor", core)
-    keep = keep + got
-    arrived = [lax.ppermute(keep[k].astype(BF), "tensor", xshift(k)) for k in range(1, nx)]
+    arrived = [lax.ppermute((keep[k] + got[k]).astype(BF), "tensor", xshift(k)) for k in range(1, nx)]
     everyone = jnp.stack(arrived, 0)
-    rows = outer(keep, everyone, own).reshape(own, rank * rank)
+    rows = outer(keep, got, everyone, own).reshape(own, rank * rank)
     stacked = jnp.concatenate([rows] + [lax.ppermute(rows, "dp", oshift(k)) for k in range(1, no)], 0)
     far_other = lax.ppermute(far_mine, "tensor", core)
 

time: 23.5 us -> 23.5 us (level)
  no operation moved by 1% of the time
where the time goes in v7:
time: 23.5 us; the launch traced here: 23.4 us
  starting transfers between devices  10.1 us (43%)
  waiting for transfers between devices  6.94 us (30%)
  Pallas kernels  3.28 us (14%)
  local copies, waits for them, and re-layouts  2.37 us (10%)
  other arithmetic  0.64 us (3%)
    ppermute x1, waiting for transfers between devices, local(): lax.ppermute((keep[k] + got[k]).astype(BF), 'tensor', xshift(k))  2.77 us
    ppermute x1, starting transfers between devices, local(): far_mine = lax.ppermute(part, 'dp', near)  2.68 us
    ppermute x1, starting transfers between devices, back(): lax.ppermute(s[k], 'dp', oshift(no - k))  2.68 us
    ppermute x1, starting transfers between devices, local(): lax.ppermute(rows, 'dp', oshift(k))  2.65 us
    pallas_call x2, Pallas kernels, project(): pl.pallas_call(functools.partial(project_kernel, nx, nt), out_shape=[shap...  2.6 us
    ppermute x1, waiting for transfers between devices, local(): lax.ppermute(rows, 'dp', oshift(k))  2.3 us
    unnamed x10, local copies, waits for them, and re-layouts  2.24 us
    ppermute x1, waiting for transfers between devices, back(): lax.ppermute(s[k], 'dp', oshift(no - k))  1.86 us
  transfers between devices with their start and end apart: 6, of which 3 were waited for; matrix products, arithmetic and copies ran while one was open for 1% of the time, Pallas kernels for 1%

profile of v7, /device:TPU:0, one launch (start us, length us, event | category | flops | bytes accessed | tf_op | source)
XLA Modules:
  0.0 23.4 jit_solution(2058959006014556681)
XLA Ops:
  0.0 0.0 copy-start
  0.0 0.0 copy-start.3
  0.0 0.0 copy-start.1
  0.0 0.0 copy-start.4
  0.0 2.2 %copy-done = bf16[8,128,2048]{2,1,0:T(8,128)(2,1)S(1)} copy-done((bf16[8,128,2048]{2,1,0:T(8,128)(2,1)S(1)}, bf16[8,128,2048]{2,1,0:T(8,128)(2,1)}, u32[]{:S(2)}) %copy-start) | copy-done | bytes 4194328
  2.2 0.0 copy-done.3
  2.2 0.0 copy-start.2
  2.2 1.3 %shard_map.56 = (f32[2,64,256]{2,1,0:T(8,128)S(1)}, f32[2,64,256]{2,1,0:T(8,128)S(1)}) custom-call(bf16[1024,2048]{1,0:T(8,128)(2,1)S(1)} %bitcast.12, bf16[64,2048]{1,0:T(8,128)(2,1)S(1)} %copy-done.3, f32[8,128]{1,0:T(8,128)S(1)} %shard_map.55.token), custom_call_target="tpu_custom_call" | custom-call | flops 268435456 | bytes 4194304 | tf_op jit(solution)/shard_map/pallas_call | solution.py:48
  3.5 0.0 copy-done.1
  3.5 0.0 copy-done.4
  3.5 1.3 %shard_map.57 = (f32[2,128,256]{2,1,0:T(8,128)S(1)}, f32[2,128,256]{2,1,0:T(8,128)S(1)}) custom-call(bf16[1024,2048]{1,0:T(8,128)(2,1)S(1)} %bitcast.13, bf16[64,2048]{1,0:T(8,128)(2,1)S(1)} %copy-done.4, f32[8,128]{1,0:T(8,128)S(1)} %shard_map.55.token, f32[2,64,256]{2,1,0:T(8,128)S(1)} %get-tuple-element.9.refs_0_, f32[2,64,256]{2,1,0:T(8,128)S(1)} %get-tuple-element.10.refs_1_), custom_call_target="tpu_custom_call" | custom-call | flops 268435456 | bytes 4194304 | tf_op jit(solution)/shard_map/pallas_call | solution.py:48
  4.8 0.5 %collective-permute-start = (f32[2,128,256]{2,1,0:T(8,128)S(1)}, f32[2,128,256]{2,1,0:T(8,128)S(1)}, u32[]{:S(2)}, u32[]{:S(2)}) collective-permute-start(f32[2,128,256]{2,1,0:T(8,128)S(1)} %get-tuple-element.12), channel_id=1, source_target_pairs={{0,1},{1,0},{2,3},{3,2},{4,5},{5,4},{6,7},{7,6},{8,9},{9,8},{10,11... | collective-permute-start | bytes 786440 | tf_op jit(solution)/shard_map/ppermute | solution.py:150
  5.4 0.0 copy-done.2
  5.4 2.7 %collective-permute-start.3 = (bf16[32,4096]{1,0:T(8,128)(2,1)S(1)}, bf16[32,4096]{1,0:T(8,128)(2,1)S(1)}, u32[]{:S(2)}, u32[]{:S(2)}) collective-permute-start(bf16[32,4096]{1,0:T(8,128)(2,1)S(1)} %constant_dynamic-slice_fusion), channel_id=1, source_target_pairs={{0,4},{4,0},{8,12},{12,8},{1,5},{5,1},{9,13},{13,9},{2,6},{6,2},{1... | collective-permute-start | bytes 786440 | tf_op jit(solution)/shard_map/ppermute | solution.py:139
  8.1 0.0 collective-permute-done.got
  8.1 1.6 %collective-permute-start.1 = (bf16[128,256]{1,0:T(8,128)(2,1)S(1)}, bf16[128,256]{1,0:T(8,128)(2,1)S(1)}, u32[]{:S(2)}, u32[]{:S(2)}) collective-permute-start(bf16[128,256]{1,0:T(8,128)(2,1)S(1)} %fusion.1), channel_id=1, source_target_pairs={{0,2},{1,3},{2,0},{3,1},{4,6},{5,7},{6,4},{7,5},{8,10},{9,11},{10,... | collective-permute-start | bytes 196616 | tf_op jit(solution)/shard_map/ppermute | solution.py:151
  9.7 2.8 %collective-permute-done.1 = bf16[128,256]{1,0:T(8,128)(2,1)S(1)} collective-permute-done((bf16[128,256]{1,0:T(8,128)(2,1)S(1)}, bf16[128,256]{1,0:T(8,128)(2,1)S(1)}, u32[]{:S(2)}, u32[]{:S(2)}) %collective-permute-start.1) | collective-permute-done | bytes 65568 | tf_op jit(solution)/shard_map/ppermute | solution.py:151
  12.4 0.2 shard_map.58
  12.7 0.1 reshape.16
  12.8 2.7 %collective-permute-start.2 = (f32[2,4096]{1,0:T(2,128)S(1)}, f32[2,4096]{1,0:T(2,128)S(1)}, u32[]{:S(2)}, u32[]{:S(2)}) collective-permute-start(f32[2,4096]{1,0:T(2,128)S(1)} %reshape.16), channel_id=1, source_target_pairs={{0,8},{4,12},{8,0},{12,4},{1,9},{5,13},{9,1},{13,5},{2,10},{6,14},... | collective-permute-start | bytes 98312 | tf_op jit(solution)/shard_map/ppermute | solution.py:154
  15.4 0.0 collective-permute-done.3.mine
  15.4 0.0 collective-permute-start.4
  15.4 2.3 %collective-permute-done.2 = f32[2,4096]{1,0:T(2,128)S(1)} collective-permute-done((f32[2,4096]{1,0:T(2,128)S(1)}, f32[2,4096]{1,0:T(2,128)S(1)}, u32[]{:S(2)}, u32[]{:S(2)}) %collective-permute-start.2) | collective-permute-done | bytes 32800 | tf_op jit(solution)/shard_map/ppermute | solution.py:154
  17.8 0.0 collective-permute-done.4.other
  17.8 0.5 %shard_map.59 = f32[2,2,128]{2,1,0:T(2,128)S(1)} custom-call(f32[4,4096]{1,0:T(4,128)S(1)} %pad_maximum_fusion.rows, bf16[64,4096]{1,0:T(8,128)(2,1)S(1)} %copy-done.2, bf16[32,4096]{1,0:T(8,128)(2,1)S(1)} %collective-permute-done.3.mine, bf16[32,4096]{1,0:T(8,128)(2,1)S(1)} %collective-permute-done.4.other), custom_call_target="tpu_custom_call" | custom-call | flops 8388608 | bytes 524288 | tf_op jit(solution)/shard_map/pallas_call | solution.py:102
  18.2 2.7 %collective-permute-start.5 = (f32[2,128]{1,0:T(2,128)S(1)}, f32[2,128]{1,0:T(2,128)S(1)}, u32[]{:S(2)}, u32[]{:S(2)}) collective-permute-start(f32[2,128]{1,0:T(2,128)S(1)} %get-tuple-element.14), channel_id=1, source_target_pairs={{0,8},{4,12},{8,0},{12,4},{1,9},{5,13},{9,1},{13,5},{2,10},{6,14},... | collective-permute-start | bytes 3080 | tf_op jit(solution)/shard_map/ppermute | solution.py:158
  20.9 1.9 %collective-permute-done.5 = f32[2,128]{1,0:T(2,128)S(1)} collective-permute-done((f32[2,128]{1,0:T(2,128)S(1)}, f32[2,128]{1,0:T(2,128)S(1)}, u32[]{:S(2)}, u32[]{:S(2)}) %collective-permute-start.5) | collective-permute-done | bytes 1056 | tf_op jit(solution)/shard_map/ppermute | solution.py:158
  22.8 0.6 %fusion.2 = f32[2,256]{1,0:T(2,128)} fusion(f32[2,2,128]{2,1,0:T(2,128)S(1)} %pad_maximum_fusion.1, pred[]{:T(512)S(6)} %eq.5), kind=kLoop, calls=%fused_computation.5 | loop fusion | flops 512 | bytes 4097 | tf_op jit(solution)/shard_map/reshape | solution.py:161
  (6 shorter events, 0.1 us)
Async XLA Ops:
  0.0 2.2 %copy-start = (bf16[8,128,2048]{2,1,0:T(8,128)(2,1)S(1)}, bf16[8,128,2048]{2,1,0:T(8,128)(2,1)}, u32[]{:S(2)}) copy-start(bf16[8,128,2048]{2,1,0:T(8,128)(2,1)} %param.6) | copy-start | bytes 12582916
  0.0 2.2 %copy-start.3 = (bf16[64,2048]{1,0:T(8,128)(2,1)S(1)}, bf16[64,2048]{1,0:T(8,128)(2,1)}, u32[]{:S(2)}) copy-start(bf16[64,2048]{1,0:T(8,128)(2,1)} %basis.2) | copy-start | bytes 786436
  0.0 3.5 %copy-start.1 = (bf16[8,128,2048]{2,1,0:T(8,128)(2,1)S(1)}, bf16[8,128,2048]{2,1,0:T(8,128)(2,1)}, u32[]{:S(2)}) copy-start(bf16[8,128,2048]{2,1,0:T(8,128)(2,1)} %param.5) | copy-start | bytes 12582916
  0.0 3.5 %copy-start.4 = (bf16[64,2048]{1,0:T(8,128)(2,1)S(1)}, bf16[64,2048]{1,0:T(8,128)(2,1)}, u32[]{:S(2)}) copy-start(bf16[64,2048]{1,0:T(8,128)(2,1)} %basis.3) | copy-start | bytes 786436
  2.2 3.2 %copy-start.2 = (bf16[64,4096]{1,0:T(8,128)(2,1)S(1)}, bf16[64,4096]{1,0:T(8,128)(2,1)}, u32[]{:S(2)}) copy-start(bf16[64,4096]{1,0:T(8,128)(2,1)} %near.1) | copy-start | bytes 1572868
  4.8 3.2 %collective-permute-start = (f32[2,128,256]{2,1,0:T(8,128)S(1)}, f32[2,128,256]{2,1,0:T(8,128)S(1)}, u32[]{:S(2)}, u32[]{:S(2)}) collective-permute-start(f32[2,128,256]{2,1,0:T(8,128)S(1)} %get-tuple-element.12), channel_id=1, source_target_pairs={{0,1},{1,0},{2,3},{3,2},{4,5},{5,4},{6,7},{7,6},{8,9},{9,8},{10,11... | collective-permute-start | bytes 786440 | tf_op jit(solution)/shard_map/ppermute | solution.py:150
  5.4 10.0 %collective-permute-start.3 = (bf16[32,4096]{1,0:T(8,128)(2,1)S(1)}, bf16[32,4096]{1,0:T(8,128)(2,1)S(1)}, u32[]{:S(2)}, u32[]{:S(2)}) collective-permute-start(bf16[32,4096]{1,0:T(8,128)(2,1)S(1)} %constant_dynamic-slice_fusion), channel_id=1, source_target_pairs={{0,4},{4,0},{8,12},{12,8},{1,5},{5,1},{9,13},{13,9},{2,6},{6,2},{1... | collective-permute-start | bytes 786440 | tf_op jit(solution)/shard_map/ppermute | solution.py:139
  8.1 4.3 %collective-permute-start.1 = (bf16[128,256]{1,0:T(8,128)(2,1)S(1)}, bf16[128,256]{1,0:T(8,128)(2,1)S(1)}, u32[]{:S(2)}, u32[]{:S(2)}) collective-permute-start(bf16[128,256]{1,0:T(8,128)(2,1)S(1)} %fusion.1), channel_id=1, source_target_pairs={{0,2},{1,3},{2,0},{3,1},{4,6},{5,7},{6,4},{7,5},{8,10},{9,11},{10,... | collective-permute-start | bytes 196616 | tf_op jit(solution)/shard_map/ppermute | solution.py:151
  12.8 5.0 %collective-permute-start.2 = (f32[2,4096]{1,0:T(2,128)S(1)}, f32[2,4096]{1,0:T(2,128)S(1)}, u32[]{:S(2)}, u32[]{:S(2)}) collective-permute-start(f32[2,4096]{1,0:T(2,128)S(1)} %reshape.16), channel_id=1, source_target_pairs={{0,8},{4,12},{8,0},{12,4},{1,9},{5,13},{9,1},{13,5},{2,10},{6,14},... | collective-permute-start | bytes 98312 | tf_op jit(solution)/shard_map/ppermute | solution.py:154
  15.4 2.3 %collective-permute-start.4 = (bf16[32,4096]{1,0:T(8,128)(2,1)S(1)}, bf16[32,4096]{1,0:T(8,128)(2,1)S(1)}, u32[]{:S(2)}, u32[]{:S(2)}) collective-permute-start(bf16[32,4096]{1,0:T(8,128)(2,1)S(1)} %collective-permute-done.3.mine), channel_id=1, source_target_pairs={{0,1},{1,0},{2,3},{3,2},{4,5},{5,4},{6,7},{7,6},{8,9},{9,8},{10,11... | collective-permute-start | bytes 786440 | tf_op jit(solution)/shard_map/ppermute | solution.py:155
  18.2 4.5 %collective-permute-start.5 = (f32[2,128]{1,0:T(2,128)S(1)}, f32[2,128]{1,0:T(2,128)S(1)}, u32[]{:S(2)}, u32[]{:S(2)}) collective-permute-start(f32[2,128]{1,0:T(2,128)S(1)} %get-tuple-element.14), channel_id=1, source_target_pairs={{0,8},{4,12},{8,0},{12,4},{1,9},{5,13},{9,1},{13,5},{2,10},{6,14},... | collective-permute-start | bytes 3080 | tf_op jit(solution)/shard_map/ppermute | solution.py:158
